TPU v7x, 32 devices: a whole 2x2x4 slice. The times are simulated.
32 devices in a mesh: groups: 2 (over y), ctx: 16 (over z, x, core).
Axes of the slice: x: 2, y: 2, z: 4, core: 2. Of those that a mesh axis runs over, the one named last changes fastest.
Arguments:
- hidden: bfloat16 [16384, 7168], P(('groups', 'ctx')), parts along dimension 0, may hold values from -6 to 6
- attn_gain: bfloat16 [7168], replicated, may hold values from 0.099609375 to 1.8984375
- w_dkv: bfloat16 [7168, 576], replicated, may hold values from -0.0625 to 0.0625
- kv_gain: bfloat16 [512], replicated, may hold values from 0.099609375 to 1.8984375
- lengths: int32 [8], P('groups'), parts along dimension 0, may hold values from 1 to 384, 512 in all
- owners: int32 [8], P('groups'), parts along dimension 0, may hold values from 0 to 3, each once
- queries: bfloat16 [8, 4, 128, 576], P('groups'), parts along dimension 0, may hold values from -60 to 60
- step_rows: bfloat16 [8, 4, 576], P('groups'), parts along dimension 0, may hold values from -12 to 12
Outputs:
- attended: bfloat16 [8, 4, 128, 512], P('groups', None, 'ctx'), parts along dimension 0
There are 2 independent parts, one for each index of `groups`. A program takes and returns all parts, laid end to end along the dimension named above; an argument that names none is the same for every part. Nothing has to cross between parts.
Inputs may be any that keep to these rules, and one draw needn't show every extreme that they name: `lengths`: each request's prompt holds 16 times its entry rows, that many on every ctx device; some entry equals 384. `owners`: every block of 4 devices decodes exactly one request.
All inputs are finite; a program needn't handle non-finite values.
Results may differ from a plain program's by a relative error of at most 0.0064.
Values may be sent and summed in bfloat16 or wider, within the bound.
No kernel may reach another device: no remote copies, remote signals or barrier semaphores. Data moves between devices by JAX's collectives and lax.ppermute only.
A program may use at most 128 MiB of HBM per device.

v0:
```python
import jax
import jax.numpy as jnp
from jax import lax
from jax.sharding import PartitionSpec as P

KVL = 512
ROPE = 64
NOPE = 128


EPSILON = 1e-06


def compress(row_block, device, attn_gain, w_dkv, kv_gain, starts, lengths):
    values = row_block.astype(jnp.float32)
    meansq = jnp.mean(values * values, axis=-1, keepdims=True)
    normed = (values * lax.rsqrt(meansq + EPSILON) * attn_gain.astype(jnp.float32)).astype(
        jnp.bfloat16
    )
    projected = jnp.dot(normed, w_dkv, preferred_element_type=jnp.float32)
    latent = projected[:, :KVL]
    latent_sq = jnp.mean(latent * latent, axis=-1, keepdims=True)
    latent = latent * lax.rsqrt(latent_sq + EPSILON) * kv_gain.astype(jnp.float32)
    local_index = jnp.arange(row_block.shape[0], dtype=jnp.int32)
    end_rows = starts + lengths
    member = (local_index[:, None] >= starts[None, :]) & (local_index[:, None] < end_rows[None, :])
    row_start = jnp.sum(jnp.where(member, starts[None, :], 0), axis=1)
    row_length = jnp.sum(jnp.where(member, lengths[None, :], 0), axis=1)
    position = (device * row_length + local_index - row_start).astype(jnp.float32)
    half_rope = ROPE // 2
    frequency = 10000.0 ** (-2.0 * jnp.arange(half_rope, dtype=jnp.float32) / ROPE)
    angles = position[:, None] * frequency[None, :]
    cosine = jnp.cos(angles)
    sine_part = jnp.sin(angles)
    first_half = projected[:, KVL : KVL + half_rope]
    second_half = projected[:, KVL + half_rope :]
    rotated = jnp.concatenate(
        [
            first_half * cosine - second_half * sine_part,
            second_half * cosine + first_half * sine_part,
        ],
        axis=-1,
    )
    return jnp.concatenate([latent, rotated], axis=-1).astype(jnp.bfloat16)


def route_tables(owners, lengths, devices, own_share):
    req_count = lengths.shape[0]
    request_ids = jnp.arange(req_count, dtype=jnp.int32)
    starts = jnp.cumsum(lengths) - lengths
    is_match = owners[None, :] == request_ids[:, None]
    block_request = jnp.sum(jnp.where(is_match, request_ids[None, :], 0), axis=1)
    dest_block = jnp.arange(devices, dtype=jnp.int32) // own_share
    in_block = dest_block[:, None] == request_ids[None, :]
    dest_request = jnp.sum(jnp.where(in_block, block_request[None, :], 0), axis=1)
    is_dest = dest_request[:, None] == request_ids[None, :]
    dest_start = jnp.sum(jnp.where(is_dest, starts[None, :], 0), axis=1)
    dest_length = jnp.sum(jnp.where(is_dest, lengths[None, :], 0), axis=1)
    return (starts, dest_start, dest_length)


def pack(row_block, first_row, dest_start, dest_length, lane_all, own_share, slot_depth):
    offsets = lane_all[:, None] + own_share * jnp.arange(slot_depth, dtype=jnp.int32)[None, :]
    row_index = dest_start[:, None] + offsets
    row_valid = (
        (offsets < dest_length[:, None])
        & (row_index >= first_row)
        & (row_index < first_row + row_block.shape[0])
    )
    picked = jnp.take(row_block, jnp.clip(row_index - first_row, 0, row_block.shape[0] - 1), axis=0)
    return jnp.where(row_valid[:, :, None], picked, jnp.zeros((), jnp.bfloat16))


def shards(hidden, attn_gain, w_dkv, kv_gain, lengths, owners, queries, step_rows):
    devices = lax.axis_size("ctx")
    device = lax.axis_index("ctx")
    req_count = lengths.shape[0]
    own_share = devices // req_count
    tokens_here = hidden.shape[0]
    most_rows = min(3 * tokens_here // req_count, tokens_here - req_count + 1)
    slot_depth = (most_rows + own_share - 1) // own_share
    starts, dest_start, dest_length = route_tables(owners, lengths, devices, own_share)
    lane_all = jnp.arange(devices, dtype=jnp.int32) % own_share
    row_block = compress(hidden, device, attn_gain, w_dkv, kv_gain, starts, lengths)
    send_all = pack(row_block, 0, dest_start, dest_length, lane_all, own_share, slot_depth)
    received = lax.all_to_all(send_all, "ctx", split_axis=0, concat_axis=0, tiled=True)
    is_mine = jnp.arange(devices, dtype=jnp.int32) == device
    own_length = jnp.sum(jnp.where(is_mine, dest_length, 0))
    lane_index = device % own_share
    own_block = device // own_share
    slot_offsets = lane_index + own_share * jnp.arange(slot_depth, dtype=jnp.int32)
    slot_valid = slot_offsets < own_length
    key_valid = jnp.broadcast_to(slot_valid[None, :], (devices, slot_depth)).reshape(-1)
    key_rows = received.reshape(-1, received.shape[-1])
    query_block = lax.dynamic_index_in_dim(queries, own_block, 0, keepdims=False)
    step_keys = lax.dynamic_index_in_dim(step_rows, own_block, 0, keepdims=False)
    step_count = query_block.shape[0]
    head_count = query_block.shape[1]
    head_local = head_count // devices
    flat_query = query_block.reshape(step_count * head_count, -1)
    every_key = jnp.concatenate([key_rows, step_keys], axis=0)
    scores = lax.dot_general(
        flat_query, every_key, (((1,), (1,)), ((), ())), preferred_element_type=jnp.float32
    )
    scores = scores * (NOPE + ROPE) ** (-0.5)
    query_step = jnp.arange(step_count * head_count, dtype=jnp.int32) // head_count
    causal = (jnp.arange(step_count, dtype=jnp.int32)[None, :] <= query_step[:, None]) & (
        lane_index == 0
    )
    prompt_mask = jnp.broadcast_to(
        key_valid[None, :], (step_count * head_count, key_valid.shape[0])
    )
    allowed = jnp.concatenate([prompt_mask, causal], axis=1)
    scores = jnp.where(allowed, scores, -1e30)
    local_peak = jnp.max(scores, axis=1)
    exponent = jnp.where(allowed, jnp.exp(scores - local_peak[:, None]), 0.0)
    local_total = jnp.sum(exponent, axis=1).reshape(step_count, head_count)
    weights = exponent.astype(jnp.bfloat16)
    mixture = jnp.dot(weights, every_key[:, :KVL], preferred_element_type=jnp.float32)
    mixture = mixture.reshape(step_count, head_count, -1)
    local_peak = local_peak.reshape(step_count, head_count)
    block_hot = jnp.arange(req_count, dtype=jnp.int32) == own_block
    peak_table = jnp.where(block_hot[:, None, None], local_peak[None], -1e30)
    peak_table = lax.pmax(peak_table, "ctx")
    row_peak = lax.dynamic_index_in_dim(peak_table, own_block, 0, keepdims=False)
    scale = jnp.exp(local_peak - row_peak)
    total_table = jnp.where(block_hot[:, None, None], (local_total * scale)[None], 0.0)
    total_table = lax.psum(total_table, "ctx")
    total_here = lax.dynamic_slice_in_dim(total_table, device * head_local, head_local, 2)
    scaled = mixture * scale[..., None]
    stacked = jnp.where(block_hot[:, None, None, None], scaled[None], 0.0)
    summed = lax.psum_scatter(stacked, "ctx", scatter_dimension=2, tiled=True)
    return (summed / total_here[..., None]).astype(jnp.bfloat16)


def solution(mesh):
    in_specs = (
        P(("groups", "ctx"), None),
        P(),
        P(),
        P(),
        P("groups"),
        P("groups"),
        P("groups", None, None, None),
        P("groups", None, None),
    )
    out_specs = P("groups", None, "ctx", None)
    return jax.shard_map(shards, mesh=mesh, in_specs=in_specs, out_specs=out_specs, check_vma=False)
```

profile of v0, /device:TPU:0, one launch (start us, length us, event | category | flops | bytes accessed | tf_op | source)
XLA Modules:
  0.0 209.3 jit_solution(12089403151688637828)
XLA Ops:
  6.5 0.0 copy-start
  6.6 1.0 reduce-window.8
  7.5 0.7 bitcast_subtract_fusion.2
  8.2 0.8 select_reduce_fusion.5
  9.0 0.7 convert_element_type.29
  9.7 0.0 copy-start.3
  9.7 0.0 copy-start.2
  9.7 4.6 %fusion = f32[512]{0:T(512)S(1)} fusion(bf16[512,7168]{1,0:T(8,128)(2,1)} %param.8), kind=kLoop, calls=%fused_computation.3 | loop fusion | flops 11009536 | bytes 7342080 | tf_op jit(solution)/shard_map/reduce_sum | solution.py:16
  14.3 0.1 select_reduce_fusion.4
  14.4 0.0 copy-done.3
  14.4 0.1 select_reduce_fusion.3
  14.5 0.1 select_reduce_fusion.1
  14.6 0.1 compare_select_fusion
  14.6 0.1 fusion.38
  14.7 0.1 reshape.330
  14.8 0.0 copy-done.2
  14.8 9.2 %fusion.3 = f32[512,576]{0,1:T(8,128)S(1)} fusion(bf16[7168,576]{0,1:T(8,128)(2,1)} %param.10, bf16[512,7168]{1,0:T(8,128)(2,1)} %param.8, f32[7168]{0:T(1024)S(1)} %convert_element_type.27, f32[512]{0:T(512)S(1)} %add_rsqrt_fusion.1), kind=kOutput, calls=%fused_computation.6 | convolution fusion | flops 4242538496 | bytes 16807936 | tf_op jit(solution)/shard_map/dot_general | solution.py:20
  24.0 0.1 multiply_reduce_fusion
  24.2 0.3 fusion.28
  24.5 0.1 multiply_convert_fusion
  24.7 0.8 pad_maximum_fusion
  25.5 1.4 copy.13
  26.9 5.6 %gather_fusion = bf16[1536,576]{1,0:T(8,128)(2,1)} fusion(bf16[512,576]{1,0:T(8,128)(2,1)S(1)} %copy.13, s32[2048]{0:T(1024)S(1)} %pad_clamp_fusion), kind=kCustom, calls=%fused_computation | custom fusion | bytes 3545088 | tf_op jit(solution)/shard_map/jit(_take)/gather | solution.py:70
  32.4 2.8 %select_select_fusion = bf16[16,96,576]{2,1,0:T(8,128)(2,1)} fusion(bf16[16,96,576]{2,1,0:T(8,128)(2,1)} %bitcast.38, pred[16,96]{1,0:T(8,128)(4,1)S(1)} %get-tuple-element.12, pred[16,96]{1,0:T(8,128)(4,1)S(1)} %get-tuple-element.11), kind=kLoop, calls=%fused_computation.19 | loop fusion | flops 1769472 | bytes 3542016 | tf_op jit(solution)/shard_map/jit(_where)/select_n | solution.py:71
  35.2 7.4 %all-to-all-start = ((bf16[16,96,576]{2,1,0:T(8,128)(2,1)}), bf16[16,96,576]{2,1,0:T(8,128)(2,1)}, u32[]{:S(2)}, u32[]{:S(2)}) async-start(bf16[16,96,576]{2,1,0:T(8,128)(2,1)} %select_select_fusion), calls=%async_computation | async-start | bytes 3932160 | tf_op jit(solution)/shard_map/all_to_all | solution.py:86
  42.6 0.0 reduce-scatter.2.cloned.1.call-start
  42.7 0.6 fusion.48
  43.3 0.7 add_compare_fusion.1
  44.0 0.1 reshape.337
  44.1 0.0 copy-done
  44.1 0.5 copy.12
  44.6 0.7 dynamic-slice_bitcast_fusion
  45.3 36.2 %all-to-all-done = bf16[16,96,576]{2,1,0:T(8,128)(2,1)} async-done(((bf16[16,96,576]{2,1,0:T(8,128)(2,1)}), bf16[16,96,576]{2,1,0:T(8,128)(2,1)}, u32[]{:S(2)}, u32[]{:S(2)}) %all-to-all-start) | async-done | bytes 1769504 | tf_op jit(solution)/shard_map/all_to_all | solution.py:86
  81.5 3.4 %fusion.53 = (f32[512]{0:T(512)S(1)}, f32[512,1540]{0,1:T(8,128)S(1)}) fusion(bf16[4,576]{1,0:T(4,128)(2,1)S(1)} %dynamic-slice_bitcast_fusion, bf16[1536,576]{1,0:T(8,128)(2,1)} %bitcast.3, bf16[72,8,4,128]{3,2,1,0:T(4,128)(2,1)S(1)} %bitcast.40, pred[512,4]{0,1:T(4,128)(4,1)S(1)} %fusion.39, pred[1540]{0:T(1024)(128)(4,1)S(1)} %pad.5.clone), kind=kOutput, calls=%fused_computation.108 | convolution fusion | flops 915030528 | bytes 5523460 | tf_op jit(solution)/shard_map/dot_general | solution.py:102
  84.9 0.0 copy-start.1
  84.9 3.8 %fusion.13 = f32[512,512]{1,0:T(8,128)S(1)} fusion(f32[512,1540]{0,1:T(8,128)S(1)} %get-tuple-element.14, pred[512,4]{0,1:T(4,128)(4,1)S(1)} %fusion.39, bf16[4,576]{1,0:T(4,128)(2,1)S(1)} %dynamic-slice_bitcast_fusion, bf16[1536,576]{1,0:T(8,128)(2,1)} %bitcast.3, f32[512]{0:T(512)S(1)} %get-tuple-element.13, pred[1540]{0:T(1024)(128)(4,1)S(1)} %pad.5.clone), kind=kOutput, calls=%fused_computation.20 | convolution fusion | flops 813711360 | bytes 5982212 | tf_op jit(solution)/shard_map/dot_general | solution.py:119
  88.8 0.0 copy-done.1
  88.8 0.1 broadcast_select_fusion.2
  88.9 39.2 %pmax.7 = f32[4,4,128]{2,1,0:T(4,128)S(1)} all-reduce(f32[4,4,128]{2,1,0:T(4,128)S(1)} %broadcast_select_fusion.2), channel_id=1, replica_groups=mesh['groups'=2,'ctx'=16] {'ctx'}, use_global_device_ids=true, to_apply=%region_11.12 | all-reduce | flops 2048 | bytes 16384 | tf_op jit(solution)/shard_map/pmax | solution.py:124
  128.1 0.1 broadcast_multiply_fusion
  128.2 2.5 %broadcast_select_fusion = f32[4,4,128,512]{3,2,1,0:T(8,128)} fusion(f32[4,128,512]{2,1,0:T(8,128)S(1)} %broadcast_multiply_fusion, pred[4]{0:T(512)(128)(4,1)S(1)} %iota_compare_fusion.6), kind=kLoop, calls=%fused_computation.15 | loop fusion | flops 1048576 | bytes 5242884 | tf_op jit(solution)/shard_map/jit(_where)/select_n | solution.py:131
  130.7 0.0 reduce-scatter.2.cloned.1.call-update
  130.8 3.0 %fusion.8 = f32[512]{0:T(512)S(1)} fusion(f32[512,1540]{0,1:T(8,128)} %copy-done.1, pred[512,4]{0,1:T(4,128)(4,1)S(1)} %fusion.39, f32[512]{0:T(512)S(1)} %get-tuple-element.13, pred[1540]{0:T(1024)(128)(4,1)S(1)} %pad.5.clone), kind=kLoop, calls=%fused_computation.13 | loop fusion | flops 3153408 | bytes 3161604 | tf_op jit(solution)/shard_map/reduce_sum | solution.py:117
  133.8 0.1 broadcast_select_fusion.1
  133.9 30.2 %psum.7 = f32[4,4,128]{2,1,0:T(4,128)S(1)} all-reduce(f32[4,4,128]{2,1,0:T(4,128)S(1)} %broadcast_select_fusion.1), channel_id=1, replica_groups=mesh['groups'=2,'ctx'=16] {'ctx'}, use_global_device_ids=true, to_apply=%region_14.15 | all-reduce | flops 2048 | bytes 16384 | tf_op jit(solution)/shard_map/psum | solution.py:128
  164.1 0.1 constant_dynamic-slice_fusion
  164.1 36.6 %reduce-scatter.2.cloned.1.call-done = f32[4,4,8,512]{3,2,1,0:T(8,128)} async-done(((f32[4,4,128,512]{3,2,1,0:T(8,128)}), f32[4,4,8,512]{3,2,1,0:T(8,128)}) %reduce-scatter.2.cloned.1.call-update) | async-done | bytes 262160 | tf_op jit(solution)/shard_map/reduce_scatter | solution.py:132
  200.7 1.7 divide_convert_fusion
  (16 shorter events, 0.2 us)
Async XLA Ops:
  6.5 37.5 %copy-start = (bf16[4,4,128,576]{2,3,1,0:T(8,128)(2,1)S(1)}, bf16[4,4,128,576]{2,3,1,0:T(8,128)(2,1)}, u32[]{:S(2)}) copy-start(bf16[4,4,128,576]{2,3,1,0:T(8,128)(2,1)} %param.14) | copy-start | bytes 7077892
  9.7 4.7 %copy-start.3 = (s32[4]{0:T(128)S(1)}, s32[4]{0:T(128)}, u32[]{:S(2)}) copy-start(s32[4]{0:T(128)} %param.12) | copy-start | bytes 52
  9.7 5.2 %copy-start.2 = (bf16[7168]{0:T(1024)(128)(2,1)S(1)}, bf16[7168]{0:T(1024)(128)(2,1)}, u32[]{:S(2)}) copy-start(bf16[7168]{0:T(1024)(128)(2,1)} %param.9) | copy-start | bytes 43012
  35.2 46.3 %all-to-all-start = ((bf16[16,96,576]{2,1,0:T(8,128)(2,1)}), bf16[16,96,576]{2,1,0:T(8,128)(2,1)}, u32[]{:S(2)}, u32[]{:S(2)}) async-start(bf16[16,96,576]{2,1,0:T(8,128)(2,1)} %select_select_fusion), calls=%async_computation | async-start | bytes 3932160 | tf_op jit(solution)/shard_map/all_to_all | solution.py:86
  42.6 158.1 %reduce-scatter.2.cloned.1.call-start = ((), (), s32[]{:S(2)}) async-start(), calls=%async_computation.2 | async-start | bytes 4456448 | tf_op jit(solution)/shard_map/reduce_scatter | solution.py:132
  84.9 3.8 %copy-start.1 = (f32[512,1540]{0,1:T(8,128)}, f32[512,1540]{0,1:T(8,128)S(1)}, u32[]{:S(2)}) copy-start(f32[512,1540]{0,1:T(8,128)S(1)} %get-tuple-element.14) | copy-start | bytes 9461764
Sparse Core Ops, SparseCore 0:
  130.9 69.8 reduce-scatter.1
where the time goes:
time: 210 us; the launch traced here: 209 us
  waiting for transfers between devices  72.8 us (35%)
  blocking collectives  69.3 us (33%)
  other arithmetic  21.3 us (10%)
  matrix products  16.5 us (8%)
  between operations  13.6 us (6%)
  local copies, waits for them, and re-layouts  8.37 us (4%)
  starting transfers between devices  7.44 us (4%)
    pmax x1, blocking collectives, shards(): peak_table = lax.pmax(peak_table, 'ctx')  39.2 us
    reduce_scatter x1, waiting for transfers between devices, shards(): summed = lax.psum_scatter(stacked, 'ctx', scatter_dimension=2, tiled=True)  36.6 us
    all_to_all x1, waiting for transfers between devices, shards(): lax.all_to_all(send_all, 'ctx', split_axis=0, concat_axis=0, tiled=True)  36.2 us
    psum x1, blocking collectives, shards(): total_table = lax.psum(total_table, 'ctx')  30.2 us
    dot_general x1, matrix products, compress(): projected = jnp.dot(normed, w_dkv, preferred_element_type=jnp.float32)  9.2 us
    all_to_all x1, starting transfers between devices, shards(): lax.all_to_all(send_all, 'ctx', split_axis=0, concat_axis=0, tiled=True)  7.4 us
    gather x1, local copies, waits for them, and re-layouts, pack(): jnp.take(row_block, jnp.clip(row_index - first_row, 0, row_block.shape[0]...  5.55 us
    reduce_sum x1, other arithmetic, compress(): meansq = jnp.mean(values * values, axis=-1, keepdims=True)  4.62 us
  transfers between devices with their start and end apart: 2, of which 2 were waited for; matrix products, arithmetic and copies ran while one was open for 3% of the time, Pallas kernels for 0%

commit v1 on v0

v1 whole, which is shorter than its diff:
```python
import functools
import math

import jax
import jax.numpy as jnp
import numpy as np
from jax import lax
from jax.experimental import pallas as pl
from jax.experimental.pallas import tpu as pltpu
from jax.sharding import PartitionSpec as P

KVL = 512
ROPE = 64
NOPE = 128
WIDTH = KVL + ROPE
EPSILON = 1e-06
SCALE = (NOPE + ROPE) ** (-0.5)
STAT_ROWS = 8
VMEM_BYTES = 48 * 1024 * 1024

NT = (((1,), (1,)), ((), ()))


def place(devices):
    cores = 2 if devices % 2 == 0 else 1
    chips = devices // cores
    along_x = max(k for k in range(1, chips + 1) if chips % k == 0 and k * k * k <= chips)
    return chips // along_x, along_x, cores


def scalars(lengths_ref, owners_ref, most):
    count = lengths_ref.shape[0]
    starts = []
    total = jnp.int32(0)
    for r in range(count):
        starts.append(total)
        total = total + lengths_ref[r]
    long_start, long_block = jnp.int32(0), jnp.int32(0)
    for r in range(count):
        is_long = lengths_ref[r] == most
        long_start = jnp.where(is_long, starts[r], long_start)
        long_block = jnp.where(is_long, owners_ref[r], long_block)
    return starts, long_start, long_block


def short_slots(lengths_ref, owners_ref, starts, long_block):
    count = lengths_ref.shape[0]
    slots = []
    for i in range(count - 1):
        block = jnp.where(long_block <= i, jnp.int32(i + 1), jnp.int32(i))
        first, rows = jnp.int32(0), jnp.int32(0)
        for r in range(count):
            is_it = owners_ref[r] == block
            first = jnp.where(is_it, starts[r], first)
            rows = jnp.where(is_it, lengths_ref[r], rows)
        slots.append((block, first, rows))
    return slots


def sin_cos(angle):
    n = jnp.round(angle * np.float32(2.0 / math.pi))
    r = ((angle - n * np.float32(1.5703125)) - n * np.float32(4.8375129699707031e-4)) - n * np.float32(
        7.5497899548918822e-8
    )
    z = r * r
    sine = ((np.float32(-1.9515295891e-4) * z + np.float32(8.3321608736e-3)) * z + np.float32(-1.6666654611e-1)) * z * r + r
    cosine = (
        ((np.float32(2.443315711809948e-5) * z + np.float32(-1.388731625493765e-3)) * z + np.float32(4.166664568298827e-2)) * z * z
        - np.float32(0.5) * z
        + np.float32(1.0)
    )
    quadrant = n.astype(jnp.int32) & 3
    odd = (quadrant & 1) == 1
    out_sine = jnp.where(odd, cosine, sine)
    out_cosine = jnp.where(odd, sine, cosine)
    out_sine = jnp.where(quadrant >= 2, -out_sine, out_sine)
    out_cosine = jnp.where((quadrant == 1) | (quadrant == 2), -out_cosine, out_cosine)
    return out_sine, out_cosine


def compress_kernel(
    most,
    chunks,
    lengths_hbm,
    owners_hbm,
    x_hbm,
    gain_hbm,
    w_hbm,
    kv_gain_hbm,
    long_ref,
    short_ref,
    x_buf,
    w_buf,
    acc,
    lengths_ref,
    owners_ref,
    gain_ref,
    kv_gain_ref,
    small,
    sem,
):
    tokens, model = x_buf.shape
    head = [
        pltpu.make_async_copy(source, target, small.at[i])
        for i, (source, target) in enumerate(
            ((lengths_hbm, lengths_ref), (owners_hbm, owners_ref), (gain_hbm, gain_ref), (kv_gain_hbm, kv_gain_ref))
        )
    ]
    copies, begin = [], 0
    for i, depth in enumerate(chunks):
        part = pl.ds(begin, depth)
        copies.append(
            (
                pltpu.make_async_copy(w_hbm.at[:, part], w_buf.at[:, part], sem.at[0, i]),
                pltpu.make_async_copy(x_hbm.at[:, part], x_buf.at[:, part], sem.at[1, i]),
            )
        )
        begin += depth
    for copy in head:
        copy.start()
    for pair in copies:
        for copy in pair:
            copy.start()
    for copy in head:
        copy.wait()

    device = lax.axis_index("ctx")
    starts, long_start, _ = scalars(lengths_ref, owners_ref, most)
    half = ROPE // 2
    token = lax.broadcasted_iota(jnp.int32, (1, tokens), 1)
    position = jnp.zeros((1, tokens), jnp.int32)
    for r in range(lengths_ref.shape[0]):
        inside = (token >= starts[r]) & (token < starts[r] + lengths_ref[r])
        position = jnp.where(inside, device * lengths_ref[r] + token - starts[r], position)
    index = lax.broadcasted_iota(jnp.int32, (half, 1), 0)
    frequency = jnp.zeros((half, 1), jnp.float32)
    for i in range(half):
        frequency = jnp.where(index == i, np.float32(10000.0 ** (-2.0 * i / ROPE)), frequency)
    sine, cosine = sin_cos(frequency * position.astype(jnp.float32))
    gain = jnp.transpose(jnp.broadcast_to(kv_gain_ref[...].astype(jnp.float32).reshape(1, KVL), (128, KVL)))
    row_gain = gain_ref[...].reshape(1, model)
    source = lax.broadcasted_iota(jnp.int32, (tokens, tokens), 0) + long_start
    source = jnp.where(source >= tokens, source - tokens, source)
    turn = (source == lax.broadcasted_iota(jnp.int32, (tokens, tokens), 1)).astype(jnp.bfloat16)

    squares = jnp.zeros((tokens, 128), jnp.float32)
    begin = 0
    for i, depth in enumerate(chunks):
        part = slice(begin, begin + depth)
        for copy in copies[i]:
            copy.wait()
        x = x_buf[:, part]
        product = lax.dot_general(w_buf[:, part], x * row_gain[:, part], NT, preferred_element_type=jnp.float32)
        if i == 0:
            acc[...] = product
        else:
            acc[...] += product
        for j in range(depth // 128):
            piece = x[:, j * 128 : (j + 1) * 128].astype(jnp.float32)
            squares = squares + piece * piece
        begin += depth
    mean = jnp.sum(jnp.transpose(squares), axis=0, keepdims=True) * np.float32(1.0 / model)
    scale = lax.rsqrt(mean + EPSILON)
    latent = acc[:KVL, :]
    latent_mean = jnp.sum(latent * latent, axis=0, keepdims=True) * (scale * scale) * np.float32(1.0 / KVL)
    latent = latent * (scale * lax.rsqrt(latent_mean + EPSILON)) * wide(gain, tokens)
    first = acc[KVL : KVL + half, :] * scale
    second = acc[KVL + half :, :] * scale
    columns = jnp.concatenate(
        [latent, first * cosine - second * sine, second * cosine + first * sine], axis=0
    ).astype(jnp.bfloat16)
    turned = lax.dot_general(turn, columns, NT, preferred_element_type=jnp.float32).astype(jnp.bfloat16)
    long_ref[...] = turned[:most]
    short_ref[...] = turned[most:]


def pick_kernel(most, sizes, lengths_ref, owners_ref, queries_hbm, long_ref, short_ref, buf, long_buf, short_buf, sem):
    zs, xs, cores = sizes
    device = lax.axis_index("ctx")
    _, _, long_block = scalars(lengths_ref, owners_ref, most)
    count, steps, _, heads = queries_hbm.shape
    local = heads // (zs * xs * cores)
    core = lax.rem(device, cores)
    here_x = lax.rem(device // cores, xs)
    here_z = device // (cores * xs)
    blocks = [long_block] + [jnp.where(long_block <= i, i + 1, i) for i in range(count - 1)]
    copies = [
        pltpu.make_async_copy(queries_hbm.at[block], buf.at[i], sem.at[i]) for i, block in enumerate(blocks)
    ]
    for copy in copies:
        copy.start()

    def head_of(rows, spread):
        row = lax.broadcasted_iota(jnp.int32, (rows, heads), 0)
        unit, inner = row // local, lax.rem(row, local)
        z = lax.rem(lax.rem(unit, zs) + here_z, zs)
        x = lax.rem(unit // zs + here_x, xs) if spread else here_x
        head = ((z * xs + x) * cores + core) * local + inner
        return (head == lax.broadcasted_iota(jnp.int32, (rows, heads), 1)).astype(jnp.bfloat16)

    long_pick, short_pick = head_of(xs * zs * local, True), head_of(zs * local, False)
    copies[0].wait()
    for t in range(steps):
        rows = lax.dot_general(long_pick, buf[0, t], NT, preferred_element_type=jnp.float32)
        for u in range(xs * zs):
            long_buf[(u * steps + t) * local : (u * steps + t + 1) * local, :] = rows[u * local : (u + 1) * local]
    long_ref[...] = long_buf[...].astype(jnp.bfloat16)
    for i in range(1, count):
        copies[i].wait()
        for t in range(steps):
            rows = lax.dot_general(short_pick, buf[i, t], NT, preferred_element_type=jnp.float32)
            for u in range(zs):
                at = ((u * (count - 1) + i - 1) * steps + t) * local
                short_buf[at : at + local, :] = rows[u * local : (u + 1) * local]
    short_ref[...] = short_buf[...].astype(jnp.bfloat16)


def as_line(column):
    return jnp.transpose(jnp.broadcast_to(column, (column.shape[0], 128)))[:8]


def as_columns(line):
    return jnp.transpose(jnp.broadcast_to(line, (128, line.shape[1])))


def stat_rows(line):
    rows = line.shape[1]
    high = line.astype(jnp.bfloat16).astype(jnp.float32)
    rest = line - high
    middle = rest.astype(jnp.bfloat16).astype(jnp.float32)
    low = rest - middle
    index = lax.broadcasted_iota(jnp.int32, (STAT_ROWS, rows), 0)
    pieces = jnp.where(index == 0, high, jnp.where(index == 1, middle, jnp.where(index == 2, low, 0.0)))
    if rows < KVL:
        pieces = jnp.concatenate([pieces, jnp.zeros((STAT_ROWS, KVL - rows), jnp.float32)], axis=1)
    return pieces


def read_line(pieces, rows):
    return pieces[0:1, :rows] + pieces[1:2, :rows] + pieces[2:3, :rows]


def wide(stat, width=KVL):
    return jnp.concatenate([stat] * (width // 128), axis=1)


def long_kernel(q_ref, key_refs, out_refs):
    keys = jnp.concatenate([ref[...] for ref in key_refs], axis=0)
    rows = q_ref.shape[0] // len(out_refs)
    scores = lax.dot_general(q_ref[...], keys, NT, preferred_element_type=jnp.float32) * SCALE
    peak = jnp.max(scores, axis=1, keepdims=True)
    weights = jnp.exp(scores - peak)
    total = jnp.sum(weights, axis=1, keepdims=True)
    mixed = jnp.dot(weights.astype(jnp.bfloat16), keys[:, :KVL], preferred_element_type=jnp.float32) / total
    lse = peak + jnp.log(total)
    for j, ref in enumerate(out_refs):
        part = slice(j * rows, (j + 1) * rows)
        ref[...] = jnp.concatenate([mixed[part], stat_rows(as_line(lse[part]))], axis=0).astype(jnp.bfloat16)


def short_kernel(most, lengths_ref, owners_ref, q_ref, key_refs, out_refs, lse_ref):
    count = lengths_ref.shape[0]
    starts, long_start, long_block = scalars(lengths_ref, owners_ref, most)
    slots = short_slots(lengths_ref, owners_ref, starts, long_block)
    keys = jnp.concatenate([ref[...] for ref in key_refs], axis=0)
    shorts = key_refs[0].shape[0]
    tokens = shorts + most
    rows = q_ref.shape[0]
    per_dest = rows // len(out_refs)
    per_slot = per_dest // (count - 1)
    scores = lax.dot_general(q_ref[...], keys, NT, preferred_element_type=jnp.float32) * SCALE
    key = lax.rem(lax.broadcasted_iota(jnp.int32, (1, keys.shape[0]), 1), shorts)
    local = key + (long_start + most)
    local = jnp.where(local >= tokens, local - tokens, local)
    slot = lax.rem(lax.broadcasted_iota(jnp.int32, (rows, 1), 0), per_dest) // per_slot
    first, stop = jnp.zeros_like(slot), jnp.zeros_like(slot)
    for i, (_, start, length) in enumerate(slots):
        first = jnp.where(slot == i, start, first)
        stop = jnp.where(slot == i, start + length, stop)
    allowed = (local >= first) & (local < stop)
    scores = jnp.where(allowed, scores, -1e30)
    peak = jnp.max(scores, axis=1, keepdims=True)
    weights = jnp.where(allowed, jnp.exp(scores - peak), 0.0)
    total = jnp.sum(weights, axis=1, keepdims=True)
    mixed = jnp.dot(weights.astype(jnp.bfloat16), keys[:, :KVL], preferred_element_type=jnp.float32) / total
    lse = peak + jnp.log(total)
    for k, ref in enumerate(out_refs):
        part = slice(k * per_dest, (k + 1) * per_dest)
        ref[...] = mixed[part].astype(jnp.bfloat16)
        lse_ref[k] = as_line(lse[part])


def merge_kernel(part_refs, lse_ref, out_refs):
    rows = part_refs[0].shape[0] - STAT_ROWS
    per_dest = rows // len(out_refs)
    parts = [ref[...].astype(jnp.float32) for ref in part_refs]
    lines = [read_line(part[rows:], rows) for part in parts]
    top = functools.reduce(jnp.maximum, lines)
    shares = [jnp.exp(line - top) for line in lines]
    whole = functools.reduce(lambda a, b: a + b, shares)
    mixed = functools.reduce(
        lambda a, b: a + b, [wide(as_columns(share / whole)) * part[:rows] for share, part in zip(shares, parts)]
    )
    lse = jnp.broadcast_to(top + jnp.log(whole), (8, rows))
    for k, ref in enumerate(out_refs):
        part = slice(k * per_dest, (k + 1) * per_dest)
        both = jnp.concatenate([lse_ref[k], lse[:, part]], axis=1)
        ref[...] = jnp.concatenate([mixed[part], stat_rows(both)], axis=0).astype(jnp.bfloat16)


def step_kernel(most, steps, lengths_ref, owners_ref, long_q_ref, short_q_ref, step_ref, after_ref, out_ref, lse_ref):
    count = lengths_ref.shape[0]
    _, _, long_block = scalars(lengths_ref, owners_ref, most)
    blocks = [jnp.where(long_block <= i, i + 1, i) for i in range(count - 1)] + [long_block]
    rows = out_ref.shape[0]
    per_slot = rows // count
    heads = per_slot // steps
    query = jnp.concatenate(
        [short_q_ref[: rows - per_slot, :].astype(jnp.float32), long_q_ref[:per_slot, :].astype(jnp.float32)], axis=0
    ).astype(jnp.bfloat16)
    keys = jnp.concatenate([step_ref[b].astype(jnp.float32) for b in blocks], axis=0).astype(jnp.bfloat16)
    scores = lax.dot_general(query, keys, NT, preferred_element_type=jnp.float32) * SCALE
    row = lax.broadcasted_iota(jnp.int32, scores.shape, 0)
    column = lax.broadcasted_iota(jnp.int32, scores.shape, 1)
    allowed = (row // per_slot == column // steps) & (lax.rem(column, steps) <= lax.rem(row, per_slot) // heads)
    scores = jnp.where(allowed, scores, -1e30)
    peak = jnp.max(scores, axis=1, keepdims=True)
    weights = jnp.where(allowed, jnp.exp(scores - peak), 0.0)
    total = jnp.sum(weights, axis=1, keepdims=True)
    out_ref[...] = jnp.dot(weights.astype(jnp.bfloat16), keys[:, :KVL], preferred_element_type=jnp.float32) / total
    lse_ref[...] = as_line(peak + jnp.log(total))


def last_kernel(most, lengths_ref, owners_ref, step_ref, step_lse_ref, short_refs, long_refs, out_ref):
    count = lengths_ref.shape[0]
    _, _, long_block = scalars(lengths_ref, owners_ref, most)
    blocks = [jnp.where(long_block <= i, i + 1, i) for i in range(count - 1)] + [long_block]
    rows, per_slot = step_ref.shape[0], long_refs[0].shape[0] - STAT_ROWS
    shorts = rows - per_slot
    longs = [ref[...].astype(jnp.float32) for ref in long_refs]
    lines = [step_lse_ref[:1]] + [read_line(part[per_slot:], rows) for part in longs]
    top = functools.reduce(jnp.maximum, lines)
    shares = [jnp.exp(line - top) for line in lines]
    whole = functools.reduce(lambda a, b: a + b, shares)
    columns = [wide(as_columns(share / whole)) for share in shares]
    step = step_ref[...]
    short, long = columns[0][:shorts] * step[:shorts], columns[0][shorts:] * step[shorts:]
    for column, ref, part in zip(columns[1:], short_refs, longs):
        short = short + column[:shorts] * ref[...].astype(jnp.float32)
        long = long + column[shorts:] * part[:per_slot]
    for i in range(count - 1):
        out_ref[blocks[i]] = short[i * per_slot : (i + 1) * per_slot].astype(jnp.bfloat16)
    out_ref[long_block] = long.astype(jnp.bfloat16)


SMEM = pl.BlockSpec(memory_space=pltpu.SMEM)
VMEM = pl.BlockSpec(memory_space=pltpu.VMEM)
HBM = pl.BlockSpec(memory_space=pl.ANY)


def params(**more):
    return pltpu.CompilerParams(vmem_limit_bytes=VMEM_BYTES, **more)


def shards(hidden, attn_gain, w_dkv, kv_gain, lengths, owners, queries, step_rows):
    devices = lax.axis_size("ctx")
    sizes = place(devices)
    zs, xs, cores = sizes
    tokens, model = hidden.shape
    count, steps, heads, _ = queries.shape
    most = min(3 * tokens // count, tokens - count + 1)
    shorts = tokens - most
    local = heads // devices
    bf16, f32 = jnp.bfloat16, jnp.float32

    def moved(dz, dx, dc):
        pairs = []
        for z in range(zs):
            for x in range(xs):
                for c in range(cores):
                    to = ((z + dz) % zs * xs + (x + dx) % xs) * cores + (c + dc) % cores
                    pairs.append(((z * xs + x) * cores + c, to))
        return pairs

    def send(value, dz=0, dx=0, dc=0):
        return lax.ppermute(value, "ctx", moved(dz, dx, dc))

    chunks = [1024] * ((model - 1024) // 1024)
    while sum(chunks) < model:
        chunks.append(min(512, model - sum(chunks)))
    long_keys, short_keys = pl.pallas_call(
        functools.partial(compress_kernel, most, chunks),
        in_specs=[HBM] * 6,
        out_specs=[VMEM, VMEM],
        out_shape=[jax.ShapeDtypeStruct((most, WIDTH), bf16), jax.ShapeDtypeStruct((shorts, WIDTH), bf16)],
        scratch_shapes=[
            pltpu.VMEM((tokens, model), bf16),
            pltpu.VMEM((WIDTH, model), bf16),
            pltpu.VMEM((WIDTH, tokens), f32),
            pltpu.SMEM(lengths.shape, lengths.dtype),
            pltpu.SMEM(owners.shape, owners.dtype),
            pltpu.VMEM(attn_gain.shape, bf16),
            pltpu.VMEM(kv_gain.shape, bf16),
            pltpu.SemaphoreType.DMA((4,)),
            pltpu.SemaphoreType.DMA((2, len(chunks))),
        ],
        compiler_params=pltpu.CompilerParams(vmem_limit_bytes=60 * 1024 * 1024),
        cost_estimate=pl.CostEstimate(
            flops=2 * tokens * model * WIDTH, bytes_accessed=2 * model * (tokens + WIDTH), transcendentals=0
        ),
        name="compress",
    )(lengths, owners, hidden, attn_gain, w_dkv.T, kv_gain)

    long_rows, short_rows = zs * xs * steps * local, zs * (count - 1) * steps * local
    long_q, short_q = pl.pallas_call(
        functools.partial(pick_kernel, most, sizes),
        in_specs=[SMEM, SMEM, HBM],
        out_specs=[VMEM, VMEM],
        out_shape=[jax.ShapeDtypeStruct((long_rows, WIDTH), bf16), jax.ShapeDtypeStruct((short_rows, WIDTH), bf16)],
        scratch_shapes=[
            pltpu.VMEM((count, steps, WIDTH, heads), bf16),
            pltpu.VMEM((long_rows, WIDTH), f32),
            pltpu.VMEM((short_rows, WIDTH), f32),
            pltpu.SemaphoreType.DMA((count,)),
        ],
        compiler_params=params(),
        cost_estimate=pl.CostEstimate(
            flops=2 * (long_rows + short_rows) * WIDTH * heads,
            bytes_accessed=2 * count * steps * WIDTH * heads,
            transcendentals=0,
        ),
        name="pick_queries",
    )(lengths, owners, queries.transpose(0, 1, 3, 2))

    short_in = [short_keys] + [send(short_keys, dx=j) for j in range(1, xs)]
    long_in = [long_keys] + [send(long_keys, dc=j) for j in range(1, cores)]
    x_rows = long_rows // xs + STAT_ROWS
    parts = pl.pallas_call(
        lambda q, *refs: long_kernel(q, refs[:cores], refs[cores:]),
        in_specs=[VMEM] * (1 + cores),
        out_specs=[VMEM] * xs,
        out_shape=[jax.ShapeDtypeStruct((x_rows, KVL), bf16)] * xs,
        compiler_params=params(),
        cost_estimate=pl.CostEstimate(
            flops=2 * long_rows * most * cores * (WIDTH + KVL), bytes_accessed=4 * most * WIDTH, transcendentals=0
        ),
        name="long_part",
    )(long_q, *long_in)
    sent = [send(parts[j], dx=j) for j in range(1, xs)]
    own, *short_in = lax.optimization_barrier((parts[0], *short_in))
    parts = [own] + sent
    short_in = short_in + [send(k, dc=j) for j in range(1, cores) for k in short_in]

    per_short, per_long = short_rows // zs, long_rows // xs // zs
    *short_parts, short_lse = pl.pallas_call(
        lambda a, b, q, *refs: short_kernel(
            most, a, b, q, refs[: len(short_in)], refs[len(short_in) : len(short_in) + zs], refs[-1]
        ),
        in_specs=[SMEM, SMEM] + [VMEM] * (1 + len(short_in)),
        out_specs=[VMEM] * (zs + 1),
        out_shape=[jax.ShapeDtypeStruct((per_short, KVL), bf16)] * zs + [jax.ShapeDtypeStruct((zs, 8, per_short), f32)],
        compiler_params=params(),
        cost_estimate=pl.CostEstimate(
            flops=2 * short_rows * shorts * len(short_in) * (WIDTH + KVL),
            bytes_accessed=4 * shorts * len(short_in) * WIDTH,
            transcendentals=0,
        ),
        name="short_part",
    )(lengths, owners, short_q, *short_in)
    short_parts = [short_parts[0]] + [send(short_parts[k], dz=k) for k in range(1, zs)]

    long_parts = pl.pallas_call(
        lambda *refs: merge_kernel(refs[:xs], refs[xs], refs[xs + 1 :]),
        in_specs=[VMEM] * (xs + 1),
        out_specs=[VMEM] * zs,
        out_shape=[jax.ShapeDtypeStruct((per_long + STAT_ROWS, KVL), bf16)] * zs,
        compiler_params=params(),
        cost_estimate=pl.CostEstimate(flops=0, bytes_accessed=2 * xs * x_rows * KVL, transcendentals=0),
        name="long_merge",
    )(*parts, short_lse)
    after = long_parts[0]
    long_parts = [after] + [send(long_parts[k], dz=k) for k in range(1, zs)]

    rows = per_short + per_long
    step_part, step_lse = pl.pallas_call(
        functools.partial(step_kernel, most, steps),
        in_specs=[SMEM, SMEM, VMEM, VMEM, VMEM, HBM],
        out_specs=[VMEM, VMEM],
        out_shape=[jax.ShapeDtypeStruct((rows, KVL), f32), jax.ShapeDtypeStruct((8, rows), f32)],
        compiler_params=params(),
        cost_estimate=pl.CostEstimate(flops=0, bytes_accessed=4 * rows * KVL, transcendentals=0),
        name="step_part",
    )(lengths, owners, long_q, short_q, step_rows, after)

    out = pl.pallas_call(
        lambda a, b, s, l, *refs: last_kernel(most, a, b, s, l, refs[:zs], refs[zs : 2 * zs], refs[2 * zs]),
        in_specs=[SMEM, SMEM] + [VMEM] * (2 + 2 * zs),
        out_specs=VMEM,
        out_shape=jax.ShapeDtypeStruct((count, steps * local, KVL), bf16),
        compiler_params=params(),
        cost_estimate=pl.CostEstimate(flops=0, bytes_accessed=2 * zs * rows * KVL, transcendentals=0),
        name="combine",
    )(lengths, owners, step_part, step_lse, *short_parts, *long_parts)
    return out.reshape(count, steps, local, KVL)


def solution(mesh):
    in_specs = (
        P(("groups", "ctx"), None),
        P(),
        P(),
        P(),
        P("groups"),
        P("groups"),
        P("groups", None, None, None),
        P("groups", None, None),
    )
    out_specs = P("groups", None, "ctx", None)
    return jax.shard_map(shards, mesh=mesh, in_specs=in_specs, out_specs=out_specs, check_vma=False)
```

time: 210 us -> 43.5 us (0.21)
  blocking collectives: 69.3 us -> 0 us
  waiting for transfers between devices: 72.8 us -> 9.06 us
  other arithmetic: 21.3 us -> 0 us
  Pallas kernels: 0 us -> 20.2 us
  matrix products: 16.5 us -> 0 us
  between operations: 13.6 us -> 0.08 us
  local copies, waits for them, and re-layouts: 8.37 us -> 1.95 us
  starting transfers between devices: 7.44 us -> 12 us
    pmax x1 -> x0, blocking collectives: 39.2 us -> none  [shards(): peak_table = lax.pmax(peak_table, 'ctx')]
    reduce_scatter x1 -> x0, waiting for transfers between devices: 36.6 us -> none  [shards(): summed = lax.psum_scatter(stacked, 'ctx', scatter_dimension=2, tiled=True)]
    all_to_all x1 -> x0, waiting for transfers between devices: 36.2 us -> none  [shards(): lax.all_to_all(send_all, 'ctx', split_axis=0, concat_axis=0, tiled=True)]
    psum x1 -> x0, blocking collectives: 30.2 us -> none  [shards(): total_table = lax.psum(total_table, 'ctx')]
    pallas_call x0 -> x7, Pallas kernels: none -> 20.2 us  [the longest x1 12.6 us: shards(): pl.pallas_call(functools.partial(compress_kernel, most, chunks), in_specs...]
    dot_general x3 -> x0, matrix products: 16.5 us -> none  [the longest x1 9.2 us: compress(): projected = jnp.dot(normed, w_dkv, preferred_element_type=jnp.float32)]
    ppermute x0 -> x11, starting transfers between devices: none -> 12 us  [send(): return lax.ppermute(value, 'ctx', moved(dz, dx, dc))]
    reduce_sum x8 -> x0, other arithmetic: 9.43 us -> none  [the longest x1 4.62 us: compress(): meansq = jnp.mean(values * values, axis=-1, keepdims=True)]
  transfers between devices with their start and end apart: 2 -> 11, of which waited for: 2 -> 4; matrix products, arithmetic and copies ran while one was open for 3% -> 0% of each run, Pallas kernels for 0% -> 14%
where the time goes in v1:
time: 43.5 us; the launch traced here: 43.3 us
  Pallas kernels  20.2 us (46%)
  starting transfers between devices  12 us (28%)
  waiting for transfers between devices  9.06 us (21%)
  local copies, waits for them, and re-layouts  1.95 us (4%)
    pallas_call x1, Pallas kernels, shards(): pl.pallas_call(functools.partial(compress_kernel, most, chunks), in_specs...  12.6 us
    ppermute x11, starting transfers between devices, send(): return lax.ppermute(value, 'ctx', moved(dz, dx, dc))  12 us
    ppermute x11, waiting for transfers between devices, send(): return lax.ppermute(value, 'ctx', moved(dz, dx, dc))  9.06 us
    pallas_call x1, Pallas kernels, shards(): pl.pallas_call(functools.partial(pick_kernel, most, sizes), in_specs=[SME...  2.41 us
    unnamed x12, local copies, waits for them, and re-layouts  1.95 us
    pallas_call x1, Pallas kernels, shards(): pl.pallas_call(lambda a, b, q, *refs: short_kernel(most, a, b, q, refs[:l...  1.67 us
    pallas_call x1, Pallas kernels, shards(): pl.pallas_call(lambda a, b, s, l, *refs: last_kernel(most, a, b, s, l, re...  1.43 us
    pallas_call x1, Pallas kernels, shards(): pl.pallas_call(functools.partial(step_kernel, most, steps), in_specs=[SME...  1.02 us
  transfers between devices with their start and end apart: 11, of which 4 were waited for; matrix products, arithmetic and copies ran while one was open for 0% of the time, Pallas kernels for 14%

profile of v1, /device:TPU:0, one launch (start us, length us, event | category | flops | bytes accessed | tf_op | source)
XLA Modules:
  0.0 43.3 jit_solution(8328884007660484321)
XLA Ops:
  0.0 0.0 copy-start
  0.0 0.0 copy-start.2
  0.0 0.0 copy-start.3
  0.0 0.0 copy-start.1
  0.0 12.6 %compress.1 = (bf16[384,576]{1,0:T(8,128)(2,1)}, bf16[128,576]{1,0:T(8,128)(2,1)}) custom-call(s32[4]{0:T(128)} %a.3, s32[4]{0:T(128)} %b.3, bf16[512,7168]{1,0:T(8,128)(2,1)} %x_hbm.1, bf16[7168]{0:T(1024)(128)(2,1)} %gain_hbm.1, bf16[576,7168]{1,0:T(8,128)(2,1)} %bitcast.4, bf16[512]{0:T(512)(128)(2,1)} %kv_gain_hbm.1), custom_call_target="tpu_custom_call" | custom-call | flops 4227858432 | bytes 15597568 | tf_op jit(solution)/shard_map/compress/pallas_call | solution.py:391
  12.6 0.5 %collective-permute-start = (bf16[384,576]{1,0:T(8,128)(2,1)}, bf16[384,576]{1,0:T(8,128)(2,1)S(1)}, u32[]{:S(2)}, u32[]{:S(2)}) collective-permute-start(bf16[384,576]{1,0:T(8,128)(2,1)} %get-tuple-element.27.refs_0_), channel_id=1, source_target_pairs={{0,1},{1,0},{2,3},{3,2},{4,5},{5,4},{6,7},{7,6},{8,9},{9,8},{10,11... | collective-permute-start | bytes 1327112 | tf_op jit(solution)/shard_map/ppermute | solution.py:386
  13.1 2.6 %collective-permute-start.1 = (bf16[128,576]{1,0:T(8,128)(2,1)}, bf16[128,576]{1,0:T(8,128)(2,1)S(1)}, u32[]{:S(2)}, u32[]{:S(2)}) collective-permute-start(bf16[128,576]{1,0:T(8,128)(2,1)} %get-tuple-element.32.refs_0_), channel_id=1, source_target_pairs={{0,2},{1,3},{2,0},{3,1},{4,6},{5,7},{6,4},{7,5},{8,10},{9,11},{10,... | collective-permute-start | bytes 442376 | tf_op jit(solution)/shard_map/ppermute | solution.py:386
  15.7 0.0 copy-done
  15.7 0.0 copy-done.2
  15.7 0.0 copy-done.3
  15.7 2.4 %pick_queries.1 = (bf16[256,576]{1,0:T(8,128)(2,1)S(1)}, bf16[384,576]{1,0:T(8,128)(2,1)S(1)}) custom-call(s32[4]{0:T(128)S(1)} %copy-done.2, s32[4]{0:T(128)S(1)} %copy-done.3, bf16[4,4,576,128]{3,2,1,0:T(8,128)(2,1)S(1)} %bitcast.3), custom_call_target="tpu_custom_call" | custom-call | flops 94371840 | bytes 2359296 | tf_op jit(solution)/shard_map/pick_queries/pallas_call | solution.py:415
  18.1 0.0 collective-permute-done.refs_1_
  18.1 0.0 copy-start.4
  18.1 1.0 %copy-done.4 = bf16[384,576]{1,0:T(8,128)(2,1)S(1)} copy-done((bf16[384,576]{1,0:T(8,128)(2,1)S(1)}, bf16[384,576]{1,0:T(8,128)(2,1)}, u32[]{:S(2)}) %copy-start.4) | copy-done | bytes 442392
  19.2 0.9 %long_part.1 = (bf16[136,512]{1,0:T(8,128)(2,1)S(1)}, bf16[136,512]{1,0:T(8,128)(2,1)S(1)}) custom-call(bf16[256,576]{1,0:T(8,128)(2,1)S(1)} %get-tuple-element.25.q.long_q_ref, bf16[384,576]{1,0:T(8,128)(2,1)S(1)} %copy-done.4, bf16[384,576]{1,0:T(8,128)(2,1)S(1)} %collective-permute-done.refs_1_), custom_call_target="tpu_custom_call" | custom-call | flops 427819008 | bytes 884736 | tf_op jit(solution)/shard_map/long_part/pallas_call | solution.py:438
  20.1 0.6 %collective-permute-done.1.refs_1_ = bf16[128,576]{1,0:T(8,128)(2,1)S(1)} collective-permute-done((bf16[128,576]{1,0:T(8,128)(2,1)}, bf16[128,576]{1,0:T(8,128)(2,1)S(1)}, u32[]{:S(2)}, u32[]{:S(2)}) %collective-permute-start.1) | collective-permute-done | bytes 147488 | tf_op jit(solution)/shard_map/ppermute | solution.py:386
  20.7 0.0 collective-permute-start.3
  20.7 0.5 %collective-permute-start.4 = (bf16[128,576]{1,0:T(8,128)(2,1)S(1)}, bf16[128,576]{1,0:T(8,128)(2,1)S(1)}, u32[]{:S(2)}, u32[]{:S(2)}) collective-permute-start(bf16[128,576]{1,0:T(8,128)(2,1)S(1)} %collective-permute-done.1.refs_1_), channel_id=1, source_target_pairs={{0,1},{1,0},{2,3},{3,2},{4,5},{5,4},{6,7},{7,6},{8,9},{9,8},{10,11... | collective-permute-start | bytes 442376 | tf_op jit(solution)/shard_map/ppermute | solution.py:386
  21.2 1.8 %collective-permute-start.2 = (bf16[136,512]{1,0:T(8,128)(2,1)S(1)}, bf16[136,512]{1,0:T(8,128)(2,1)S(1)}, u32[]{:S(2)}, u32[]{:S(2)}) collective-permute-start(bf16[136,512]{1,0:T(8,128)(2,1)S(1)} %get-tuple-element.31), channel_id=1, source_target_pairs={{0,2},{1,3},{2,0},{3,1},{4,6},{5,7},{6,4},{7,5},{8,10},{9,11},{10,... | collective-permute-start | bytes 417800 | tf_op jit(solution)/shard_map/ppermute | solution.py:386
  23.0 0.0 collective-permute-done.3.refs_2_
  23.0 0.0 collective-permute-done.4.refs_3_
  23.0 0.0 copy-start.5
  23.0 0.9 %copy-done.5 = bf16[128,576]{1,0:T(8,128)(2,1)S(1)} copy-done((bf16[128,576]{1,0:T(8,128)(2,1)S(1)}, bf16[128,576]{1,0:T(8,128)(2,1)}, u32[]{:S(2)}) %copy-start.5) | copy-done | bytes 147480
  23.9 1.7 %short_part.1 = (bf16[96,512]{1,0:T(8,128)(2,1)S(1)}, bf16[96,512]{1,0:T(8,128)(2,1)S(1)}, bf16[96,512]{1,0:T(8,128)(2,1)S(1)}, bf16[96,512]{1,0:T(8,128)(2,1)S(1)}, f32[4,8,96]{2,1,0:T(8,128)S(1)}) custom-call(s32[4]{0:T(128)S(1)} %copy-done.2, s32[4]{0:T(128)S(1)} %copy-done.3, bf16[384,576]{1,0:T(8,128)(2,1)S(1)} %get-tuple-element.26.q.short_q_ref, ...), custom_call_target="tpu_custom_call" | custom-call | flops 427819008 | bytes 1179648 | tf_op jit(solution)/shard_map/short_part/pallas_call | solution.py:455
  25.6 1.6 %collective-permute-start.5 = (bf16[96,512]{1,0:T(8,128)(2,1)S(1)}, bf16[96,512]{1,0:T(8,128)(2,1)S(1)}, u32[]{:S(2)}, u32[]{:S(2)}) collective-permute-start(bf16[96,512]{1,0:T(8,128)(2,1)S(1)} %get-tuple-element.39), channel_id=1, source_target_pairs={{0,4},{1,5},{2,6},{3,7},{4,8},{5,9},{6,10},{7,11},{8,12},{9,13},{1... | collective-permute-start | bytes 294920 | tf_op jit(solution)/shard_map/ppermute | solution.py:386
  27.2 2.6 %collective-permute-start.6 = (bf16[96,512]{1,0:T(8,128)(2,1)S(1)}, bf16[96,512]{1,0:T(8,128)(2,1)S(1)}, u32[]{:S(2)}, u32[]{:S(2)}) collective-permute-start(bf16[96,512]{1,0:T(8,128)(2,1)S(1)} %get-tuple-element.40), channel_id=1, source_target_pairs={{0,8},{1,9},{2,10},{3,11},{4,12},{5,13},{6,14},{7,15},{8,0},{9,1},... | collective-permute-start | bytes 294920 | tf_op jit(solution)/shard_map/ppermute | solution.py:386
  29.8 1.3 %collective-permute-start.7 = (bf16[96,512]{1,0:T(8,128)(2,1)S(1)}, bf16[96,512]{1,0:T(8,128)(2,1)S(1)}, u32[]{:S(2)}, u32[]{:S(2)}) collective-permute-start(bf16[96,512]{1,0:T(8,128)(2,1)S(1)} %get-tuple-element.41), channel_id=1, source_target_pairs={{0,12},{1,13},{2,14},{3,15},{4,0},{5,1},{6,2},{7,3},{8,4},{9,5},{1... | collective-permute-start | bytes 294920 | tf_op jit(solution)/shard_map/ppermute | solution.py:386
  31.1 0.0 collective-permute-done.2.refs_1_
  31.1 0.2 long_merge.1
  31.3 0.7 %collective-permute-start.8 = (bf16[40,512]{1,0:T(8,128)(2,1)S(1)}, bf16[40,512]{1,0:T(8,128)(2,1)S(1)}, u32[]{:S(2)}, u32[]{:S(2)}) collective-permute-start(bf16[40,512]{1,0:T(8,128)(2,1)S(1)} %get-tuple-element.42), channel_id=1, source_target_pairs={{0,4},{1,5},{2,6},{3,7},{4,8},{5,9},{6,10},{7,11},{8,12},{9,13},{1... | collective-permute-start | bytes 122888 | tf_op jit(solution)/shard_map/ppermute | solution.py:386
  32.1 0.3 collective-permute-start.9
  32.4 5.3 %collective-permute-done.8.refs_5_ = bf16[40,512]{1,0:T(8,128)(2,1)S(1)} collective-permute-done((bf16[40,512]{1,0:T(8,128)(2,1)S(1)}, bf16[40,512]{1,0:T(8,128)(2,1)S(1)}, u32[]{:S(2)}, u32[]{:S(2)}) %collective-permute-start.8) | collective-permute-done | bytes 40992 | tf_op jit(solution)/shard_map/ppermute | solution.py:386
  37.7 0.0 collective-permute-start.10
  37.7 0.0 copy-done.1
  37.7 1.0 %step_part.1 = (f32[128,512]{1,0:T(8,128)S(1)}, f32[8,128]{1,0:T(8,128)S(1)}) custom-call(s32[4]{0:T(128)S(1)} %copy-done.2, s32[4]{0:T(128)S(1)} %copy-done.3, bf16[256,576]{1,0:T(8,128)(2,1)S(1)} %get-tuple-element.25.q.long_q_ref, bf16[384,576]{1,0:T(8,128)(2,1)S(1)} %get-tuple-element.26.q.short_q_ref, bf16[4,4,576]{2,1,0:T(4,128)(2,1)S(1)} %copy-done.1, ...), custom_call_target="tpu_custom_call" | custom-call | bytes 262144 | tf_op jit(solution)/shard_map/step_part/pallas_call | solution.py:485
  38.7 2.5 %collective-permute-done.9.refs_6_ = bf16[40,512]{1,0:T(8,128)(2,1)S(1)} collective-permute-done((bf16[40,512]{1,0:T(8,128)(2,1)S(1)}, bf16[40,512]{1,0:T(8,128)(2,1)S(1)}, u32[]{:S(2)}, u32[]{:S(2)}) %collective-permute-start.9) | collective-permute-done | bytes 40992 | tf_op jit(solution)/shard_map/ppermute | solution.py:386
  41.2 0.7 %collective-permute-done.10.refs_7_ = bf16[40,512]{1,0:T(8,128)(2,1)S(1)} collective-permute-done((bf16[40,512]{1,0:T(8,128)(2,1)S(1)}, bf16[40,512]{1,0:T(8,128)(2,1)S(1)}, u32[]{:S(2)}, u32[]{:S(2)}) %collective-permute-start.10) | collective-permute-done | bytes 40992 | tf_op jit(solution)/shard_map/ppermute | solution.py:386
  41.9 0.0 collective-permute-done.5.refs_1_
  41.9 0.0 collective-permute-done.6.refs_2_
  41.9 0.0 collective-permute-done.7.refs_3_
  41.9 1.4 %combine.1 = bf16[4,32,512]{2,1,0:T(8,128)(2,1)} custom-call(s32[4]{0:T(128)S(1)} %copy-done.2, s32[4]{0:T(128)S(1)} %copy-done.3, f32[128,512]{1,0:T(8,128)S(1)} %get-tuple-element.36.s, f32[8,128]{1,0:T(8,128)S(1)} %get-tuple-element.37.l, bf16[96,512]{1,0:T(8,128)(2,1)S(1)} %get-tuple-element.38.refs_0_, ...), custom_call_target="tpu_custom_call" | custom-call | bytes 524288 | tf_op jit(solution)/shard_map/combine/pallas_call | solution.py:495
Async XLA Ops:
  0.0 15.7 %copy-start = (bf16[4,4,128,576]{2,3,1,0:T(8,128)(2,1)S(1)}, bf16[4,4,128,576]{2,3,1,0:T(8,128)(2,1)}, u32[]{:S(2)}) copy-start(bf16[4,4,128,576]{2,3,1,0:T(8,128)(2,1)} %param.14) | copy-start | bytes 7077892
  0.0 15.7 %copy-start.2 = (s32[4]{0:T(128)S(1)}, s32[4]{0:T(128)}, u32[]{:S(2)}) copy-start(s32[4]{0:T(128)} %a.3) | copy-start | bytes 52
  0.0 15.7 %copy-start.3 = (s32[4]{0:T(128)S(1)}, s32[4]{0:T(128)}, u32[]{:S(2)}) copy-start(s32[4]{0:T(128)} %b.3) | copy-start | bytes 52
  0.0 37.7 %copy-start.1 = (bf16[4,4,576]{2,1,0:T(4,128)(2,1)S(1)}, bf16[4,4,576]{2,1,0:T(4,128)(2,1)}, u32[]{:S(2)}) copy-start(bf16[4,4,576]{2,1,0:T(4,128)(2,1)} %step_ref.1) | copy-start | bytes 55300
  12.6 5.5 %collective-permute-start = (bf16[384,576]{1,0:T(8,128)(2,1)}, bf16[384,576]{1,0:T(8,128)(2,1)S(1)}, u32[]{:S(2)}, u32[]{:S(2)}) collective-permute-start(bf16[384,576]{1,0:T(8,128)(2,1)} %get-tuple-element.27.refs_0_), channel_id=1, source_target_pairs={{0,1},{1,0},{2,3},{3,2},{4,5},{5,4},{6,7},{7,6},{8,9},{9,8},{10,11... | collective-permute-start | bytes 1327112 | tf_op jit(solution)/shard_map/ppermute | solution.py:386
  13.1 7.6 %collective-permute-start.1 = (bf16[128,576]{1,0:T(8,128)(2,1)}, bf16[128,576]{1,0:T(8,128)(2,1)S(1)}, u32[]{:S(2)}, u32[]{:S(2)}) collective-permute-start(bf16[128,576]{1,0:T(8,128)(2,1)} %get-tuple-element.32.refs_0_), channel_id=1, source_target_pairs={{0,2},{1,3},{2,0},{3,1},{4,6},{5,7},{6,4},{7,5},{8,10},{9,11},{10,... | collective-permute-start | bytes 442376 | tf_op jit(solution)/shard_map/ppermute | solution.py:386
  18.1 1.0 %copy-start.4 = (bf16[384,576]{1,0:T(8,128)(2,1)S(1)}, bf16[384,576]{1,0:T(8,128)(2,1)}, u32[]{:S(2)}) copy-start(bf16[384,576]{1,0:T(8,128)(2,1)} %get-tuple-element.27.refs_0_) | copy-start | bytes 1327108
  20.7 2.3 %collective-permute-start.3 = (bf16[128,576]{1,0:T(8,128)(2,1)}, bf16[128,576]{1,0:T(8,128)(2,1)S(1)}, u32[]{:S(2)}, u32[]{:S(2)}) collective-permute-start(bf16[128,576]{1,0:T(8,128)(2,1)} %get-tuple-element.32.refs_0_), channel_id=1, source_target_pairs={{0,1},{1,0},{2,3},{3,2},{4,5},{5,4},{6,7},{7,6},{8,9},{9,8},{10,11... | collective-permute-start | bytes 442376 | tf_op jit(solution)/shard_map/ppermute | solution.py:386
  20.7 2.3 %collective-permute-start.4 = (bf16[128,576]{1,0:T(8,128)(2,1)S(1)}, bf16[128,576]{1,0:T(8,128)(2,1)S(1)}, u32[]{:S(2)}, u32[]{:S(2)}) collective-permute-start(bf16[128,576]{1,0:T(8,128)(2,1)S(1)} %collective-permute-done.1.refs_1_), channel_id=1, source_target_pairs={{0,1},{1,0},{2,3},{3,2},{4,5},{5,4},{6,7},{7,6},{8,9},{9,8},{10,11... | collective-permute-start | bytes 442376 | tf_op jit(solution)/shard_map/ppermute | solution.py:386
  21.2 9.9 %collective-permute-start.2 = (bf16[136,512]{1,0:T(8,128)(2,1)S(1)}, bf16[136,512]{1,0:T(8,128)(2,1)S(1)}, u32[]{:S(2)}, u32[]{:S(2)}) collective-permute-start(bf16[136,512]{1,0:T(8,128)(2,1)S(1)} %get-tuple-element.31), channel_id=1, source_target_pairs={{0,2},{1,3},{2,0},{3,1},{4,6},{5,7},{6,4},{7,5},{8,10},{9,11},{10,... | collective-permute-start | bytes 417800 | tf_op jit(solution)/shard_map/ppermute | solution.py:386
  23.0 0.9 %copy-start.5 = (bf16[128,576]{1,0:T(8,128)(2,1)S(1)}, bf16[128,576]{1,0:T(8,128)(2,1)}, u32[]{:S(2)}) copy-start(bf16[128,576]{1,0:T(8,128)(2,1)} %get-tuple-element.32.refs_0_) | copy-start | bytes 442372
  25.6 16.3 %collective-permute-start.5 = (bf16[96,512]{1,0:T(8,128)(2,1)S(1)}, bf16[96,512]{1,0:T(8,128)(2,1)S(1)}, u32[]{:S(2)}, u32[]{:S(2)}) collective-permute-start(bf16[96,512]{1,0:T(8,128)(2,1)S(1)} %get-tuple-element.39), channel_id=1, source_target_pairs={{0,4},{1,5},{2,6},{3,7},{4,8},{5,9},{6,10},{7,11},{8,12},{9,13},{1... | collective-permute-start | bytes 294920 | tf_op jit(solution)/shard_map/ppermute | solution.py:386
  27.2 14.7 %collective-permute-start.6 = (bf16[96,512]{1,0:T(8,128)(2,1)S(1)}, bf16[96,512]{1,0:T(8,128)(2,1)S(1)}, u32[]{:S(2)}, u32[]{:S(2)}) collective-permute-start(bf16[96,512]{1,0:T(8,128)(2,1)S(1)} %get-tuple-element.40), channel_id=1, source_target_pairs={{0,8},{1,9},{2,10},{3,11},{4,12},{5,13},{6,14},{7,15},{8,0},{9,1},... | collective-permute-start | bytes 294920 | tf_op jit(solution)/shard_map/ppermute | solution.py:386
  29.8 12.1 %collective-permute-start.7 = (bf16[96,512]{1,0:T(8,128)(2,1)S(1)}, bf16[96,512]{1,0:T(8,128)(2,1)S(1)}, u32[]{:S(2)}, u32[]{:S(2)}) collective-permute-start(bf16[96,512]{1,0:T(8,128)(2,1)S(1)} %get-tuple-element.41), channel_id=1, source_target_pairs={{0,12},{1,13},{2,14},{3,15},{4,0},{5,1},{6,2},{7,3},{8,4},{9,5},{1... | collective-permute-start | bytes 294920 | tf_op jit(solution)/shard_map/ppermute | solution.py:386
  31.3 6.4 %collective-permute-start.8 = (bf16[40,512]{1,0:T(8,128)(2,1)S(1)}, bf16[40,512]{1,0:T(8,128)(2,1)S(1)}, u32[]{:S(2)}, u32[]{:S(2)}) collective-permute-start(bf16[40,512]{1,0:T(8,128)(2,1)S(1)} %get-tuple-element.42), channel_id=1, source_target_pairs={{0,4},{1,5},{2,6},{3,7},{4,8},{5,9},{6,10},{7,11},{8,12},{9,13},{1... | collective-permute-start | bytes 122888 | tf_op jit(solution)/shard_map/ppermute | solution.py:386
  32.1 9.2 %collective-permute-start.9 = (bf16[40,512]{1,0:T(8,128)(2,1)S(1)}, bf16[40,512]{1,0:T(8,128)(2,1)S(1)}, u32[]{:S(2)}, u32[]{:S(2)}) collective-permute-start(bf16[40,512]{1,0:T(8,128)(2,1)S(1)} %get-tuple-element.43), channel_id=1, source_target_pairs={{0,8},{1,9},{2,10},{3,11},{4,12},{5,13},{6,14},{7,15},{8,0},{9,1},... | collective-permute-start | bytes 122888 | tf_op jit(solution)/shard_map/ppermute | solution.py:386
  37.7 4.2 %collective-permute-start.10 = (bf16[40,512]{1,0:T(8,128)(2,1)S(1)}, bf16[40,512]{1,0:T(8,128)(2,1)S(1)}, u32[]{:S(2)}, u32[]{:S(2)}) collective-permute-start(bf16[40,512]{1,0:T(8,128)(2,1)S(1)} %get-tuple-element.44), channel_id=1, source_target_pairs={{0,12},{1,13},{2,14},{3,15},{4,0},{5,1},{6,2},{7,3},{8,4},{9,5},{1... | collective-permute-start | bytes 122888 | tf_op jit(solution)/shard_map/ppermute | solution.py:386

commit v2 on v1

--- a/solution.py
+++ b/solution.py
@@ -16,6 +16,7 @@
 EPSILON = 1e-06
 SCALE = (NOPE + ROPE) ** (-0.5)
 STAT_ROWS = 8
+PACK = KVL // ROPE
 VMEM_BYTES = 48 * 1024 * 1024
 
 NT = (((1,), (1,)), ((), ()))
@@ -39,7 +40,8 @@
     for r in range(count):
         is_long = lengths_ref[r] == most
         long_start = jnp.where(is_long, starts[r], long_start)
-        long_block = jnp.where(is_long, owners_ref[r], long_block)
+        if owners_ref is not None:
+            long_block = jnp.where(is_long, owners_ref[r], long_block)
     return starts, long_start, long_block
 
 
@@ -82,18 +84,16 @@
     most,
     chunks,
     lengths_hbm,
-    owners_hbm,
     x_hbm,
     gain_hbm,
     w_hbm,
     kv_gain_hbm,
-    long_ref,
+    rows_ref,
     short_ref,
     x_buf,
     w_buf,
     acc,
     lengths_ref,
-    owners_ref,
     gain_ref,
     kv_gain_ref,
     small,
@@ -103,7 +103,7 @@
     head = [
         pltpu.make_async_copy(source, target, small.at[i])
         for i, (source, target) in enumerate(
-            ((lengths_hbm, lengths_ref), (owners_hbm, owners_ref), (gain_hbm, gain_ref), (kv_gain_hbm, kv_gain_ref))
+            ((lengths_hbm, lengths_ref), (gain_hbm, gain_ref), (kv_gain_hbm, kv_gain_ref))
         )
     ]
     copies, begin = [], 0
@@ -118,14 +118,16 @@
         begin += depth
     for copy in head:
         copy.start()
-    for pair in copies:
+    for copy in copies[0] + copies[1]:
+        copy.start()
+    for copy in head:
+        copy.wait()
+    for pair in copies[2:]:
         for copy in pair:
             copy.start()
-    for copy in head:
-        copy.wait()
 
     device = lax.axis_index("ctx")
-    starts, long_start, _ = scalars(lengths_ref, owners_ref, most)
+    starts, long_start, _ = scalars(lengths_ref, None, most)
     half = ROPE // 2
     token = lax.broadcasted_iota(jnp.int32, (1, tokens), 1)
     position = jnp.zeros((1, tokens), jnp.int32)
@@ -169,15 +171,34 @@
     columns = jnp.concatenate(
         [latent, first * cosine - second * sine, second * cosine + first * sine], axis=0
     ).astype(jnp.bfloat16)
-    turned = lax.dot_general(turn, columns, NT, preferred_element_type=jnp.float32).astype(jnp.bfloat16)
-    long_ref[...] = turned[:most]
-    short_ref[...] = turned[most:]
-
-
-def pick_kernel(most, sizes, lengths_ref, owners_ref, queries_hbm, long_ref, short_ref, buf, long_buf, short_buf, sem):
+    turned = lax.dot_general(turn, columns, NT, preferred_element_type=jnp.float32)
+    long, short = packed_rows(turned[:most]), packed_rows(turned[most:])
+    rows_ref[...] = jnp.concatenate([long, short], axis=0).astype(jnp.bfloat16)
+    short_ref[...] = short.astype(jnp.bfloat16)
+
+
+def packed_rows(rows):
+    deep = rows.shape[0] // PACK
+    rotary = [rows[i * deep : (i + 1) * deep, KVL:] for i in range(PACK)]
+    return jnp.concatenate([rows[:, :KVL], jnp.concatenate(rotary, axis=1)], axis=0)
+
+
+def unpacked(ref, begin, rows):
+    deep = rows // PACK
+    after = begin + rows
+    rotary = [ref[after : after + deep, i * ROPE : (i + 1) * ROPE] for i in range(PACK)]
+    return ref[begin:after, :], jnp.concatenate(rotary, axis=0)
+
+
+def score(q_ref, latent, rotary):
+    scores = lax.dot_general(q_ref[:, :KVL], latent, NT, preferred_element_type=jnp.float32)
+    return (scores + lax.dot_general(q_ref[:, KVL:], rotary, NT, preferred_element_type=jnp.float32)) * SCALE
+
+
+def pick_kernel(most, sizes, lengths_ref, owners_ref, queries_hbm, long_ref, short_ref, mask_ref, order_ref, buf, long_buf, short_buf, sem):
     zs, xs, cores = sizes
     device = lax.axis_index("ctx")
-    _, _, long_block = scalars(lengths_ref, owners_ref, most)
+    starts, long_start, long_block = scalars(lengths_ref, owners_ref, most)
     count, steps, _, heads = queries_hbm.shape
     local = heads // (zs * xs * cores)
     core = lax.rem(device, cores)
@@ -199,6 +220,18 @@
         return (head == lax.broadcasted_iota(jnp.int32, (rows, heads), 1)).astype(jnp.bfloat16)
 
     long_pick, short_pick = head_of(xs * zs * local, True), head_of(zs * local, False)
+    shape = mask_ref.shape
+    local_row = lax.broadcasted_iota(jnp.int32, shape, 1) + (long_start + most)
+    local_row = jnp.where(local_row >= shape[1] + most, local_row - (shape[1] + most), local_row)
+    slot = lax.broadcasted_iota(jnp.int32, shape, 0) // (steps * local)
+    mask = jnp.zeros(shape, jnp.float32)
+    for i, (_, start, length) in enumerate(short_slots(lengths_ref, owners_ref, starts, long_block)):
+        inside = (slot == i) & (local_row >= start) & (local_row < start + length)
+        mask = jnp.where(inside, 1.0, mask)
+    mask_ref[...] = mask
+    row = lax.broadcasted_iota(jnp.int32, order_ref.shape, 0)
+    marked = (row == long_block) | ((row >= count) & (row - count > long_block))
+    order_ref[...] = jnp.where(marked, 1.0, 0.0)
     copies[0].wait()
     for t in range(steps):
         rows = lax.dot_general(long_pick, buf[0, t], NT, preferred_element_type=jnp.float32)
@@ -244,45 +277,36 @@
     return jnp.concatenate([stat] * (width // 128), axis=1)
 
 
-def long_kernel(q_ref, key_refs, out_refs):
-    keys = jnp.concatenate([ref[...] for ref in key_refs], axis=0)
+def long_kernel(most, q_ref, key_refs, out_refs):
+    keys = [unpacked(ref, 0, most) for ref in key_refs]
+    latent, rotary = (jnp.concatenate(part, axis=0) for part in zip(*keys))
     rows = q_ref.shape[0] // len(out_refs)
-    scores = lax.dot_general(q_ref[...], keys, NT, preferred_element_type=jnp.float32) * SCALE
+    scores = score(q_ref, latent, rotary)
     peak = jnp.max(scores, axis=1, keepdims=True)
     weights = jnp.exp(scores - peak)
     total = jnp.sum(weights, axis=1, keepdims=True)
-    mixed = jnp.dot(weights.astype(jnp.bfloat16), keys[:, :KVL], preferred_element_type=jnp.float32) / total
+    mixed = jnp.dot(weights.astype(jnp.bfloat16), latent, preferred_element_type=jnp.float32) / total
     lse = peak + jnp.log(total)
     for j, ref in enumerate(out_refs):
         part = slice(j * rows, (j + 1) * rows)
         ref[...] = jnp.concatenate([mixed[part], stat_rows(as_line(lse[part]))], axis=0).astype(jnp.bfloat16)
 
 
-def short_kernel(most, lengths_ref, owners_ref, q_ref, key_refs, out_refs, lse_ref):
-    count = lengths_ref.shape[0]
-    starts, long_start, long_block = scalars(lengths_ref, owners_ref, most)
-    slots = short_slots(lengths_ref, owners_ref, starts, long_block)
-    keys = jnp.concatenate([ref[...] for ref in key_refs], axis=0)
-    shorts = key_refs[0].shape[0]
-    tokens = shorts + most
-    rows = q_ref.shape[0]
-    per_dest = rows // len(out_refs)
-    per_slot = per_dest // (count - 1)
-    scores = lax.dot_general(q_ref[...], keys, NT, preferred_element_type=jnp.float32) * SCALE
-    key = lax.rem(lax.broadcasted_iota(jnp.int32, (1, keys.shape[0]), 1), shorts)
-    local = key + (long_start + most)
-    local = jnp.where(local >= tokens, local - tokens, local)
-    slot = lax.rem(lax.broadcasted_iota(jnp.int32, (rows, 1), 0), per_dest) // per_slot
-    first, stop = jnp.zeros_like(slot), jnp.zeros_like(slot)
-    for i, (_, start, length) in enumerate(slots):
-        first = jnp.where(slot == i, start, first)
-        stop = jnp.where(slot == i, start + length, stop)
-    allowed = (local >= first) & (local < stop)
+def short_kernel(most, q_ref, mask_ref, row_refs, packed_refs, out_refs, lse_ref):
+    tokens = row_refs[0].shape[0] * PACK // (PACK + 1)
+    shorts = tokens - most
+    begin = most + most // PACK
+    keys = [unpacked(ref, begin, shorts) for ref in row_refs] + [unpacked(ref, 0, shorts) for ref in packed_refs]
+    latent, rotary = (jnp.concatenate(part, axis=0) for part in zip(*keys))
+    per_dest = mask_ref.shape[0]
+    scores = score(q_ref, latent, rotary)
+    allowed = jnp.concatenate([mask_ref[...]] * len(keys), axis=1)
+    allowed = jnp.concatenate([allowed] * len(out_refs), axis=0) > 0.0
     scores = jnp.where(allowed, scores, -1e30)
     peak = jnp.max(scores, axis=1, keepdims=True)
     weights = jnp.where(allowed, jnp.exp(scores - peak), 0.0)
     total = jnp.sum(weights, axis=1, keepdims=True)
-    mixed = jnp.dot(weights.astype(jnp.bfloat16), keys[:, :KVL], preferred_element_type=jnp.float32) / total
+    mixed = jnp.dot(weights.astype(jnp.bfloat16), latent, preferred_element_type=jnp.float32) / total
     lse = peak + jnp.log(total)
     for k, ref in enumerate(out_refs):
         part = slice(k * per_dest, (k + 1) * per_dest)
@@ -331,10 +355,8 @@
     lse_ref[...] = as_line(peak + jnp.log(total))
 
 
-def last_kernel(most, lengths_ref, owners_ref, step_ref, step_lse_ref, short_refs, long_refs, out_ref):
-    count = lengths_ref.shape[0]
-    _, _, long_block = scalars(lengths_ref, owners_ref, most)
-    blocks = [jnp.where(long_block <= i, i + 1, i) for i in range(count - 1)] + [long_block]
+def last_kernel(order_ref, step_ref, step_lse_ref, short_refs, long_refs, out_ref):
+    count = out_ref.shape[0]
     rows, per_slot = step_ref.shape[0], long_refs[0].shape[0] - STAT_ROWS
     shorts = rows - per_slot
     longs = [ref[...].astype(jnp.float32) for ref in long_refs]
@@ -348,9 +370,12 @@
     for column, ref, part in zip(columns[1:], short_refs, longs):
         short = short + column[:shorts] * ref[...].astype(jnp.float32)
         long = long + column[shorts:] * part[:per_slot]
-    for i in range(count - 1):
-        out_ref[blocks[i]] = short[i * per_slot : (i + 1) * per_slot].astype(jnp.bfloat16)
-    out_ref[long_block] = long.astype(jnp.bfloat16)
+    slots = [short[i * per_slot : (i + 1) * per_slot] for i in range(count - 1)]
+    order = order_ref[...]
+    for b in range(count):
+        is_long, behind = wide(order[b : b + 1]) > 0.0, wide(order[count + b : count + b + 1]) > 0.0
+        block = jnp.where(behind, slots[max(b - 1, 0)], slots[min(b, count - 2)])
+        out_ref[b] = jnp.where(is_long, long, block).astype(jnp.bfloat16)
 
 
 SMEM = pl.BlockSpec(memory_space=pltpu.SMEM)
@@ -373,50 +398,57 @@
     local = heads // devices
     bf16, f32 = jnp.bfloat16, jnp.float32
 
-    def moved(dz, dx, dc):
-        pairs = []
-        for z in range(zs):
-            for x in range(xs):
-                for c in range(cores):
-                    to = ((z + dz) % zs * xs + (x + dx) % xs) * cores + (c + dc) % cores
-                    pairs.append(((z * xs + x) * cores + c, to))
-        return pairs
-
-    def send(value, dz=0, dx=0, dc=0):
-        return lax.ppermute(value, "ctx", moved(dz, dx, dc))
+    def send(value, by_z=0, by_x=0, by_core=0):
+        def device(z, x, c):
+            return (z % zs * xs + x % xs) * cores + c % cores
+
+        pairs = [
+            (device(z, x, c), device(z + by_z, x + by_x, c + by_core))
+            for z in range(zs)
+            for x in range(xs)
+            for c in range(cores)
+        ]
+        return lax.ppermute(value, "ctx", pairs)
 
     chunks = [1024] * ((model - 1024) // 1024)
     while sum(chunks) < model:
         chunks.append(min(512, model - sum(chunks)))
-    long_keys, short_keys = pl.pallas_call(
+    row_keys, short_keys = pl.pallas_call(
         functools.partial(compress_kernel, most, chunks),
-        in_specs=[HBM] * 6,
+        in_specs=[HBM] * 5,
         out_specs=[VMEM, VMEM],
-        out_shape=[jax.ShapeDtypeStruct((most, WIDTH), bf16), jax.ShapeDtypeStruct((shorts, WIDTH), bf16)],
+        out_shape=[
+            jax.ShapeDtypeStruct((tokens + tokens // PACK, KVL), bf16),
+            jax.ShapeDtypeStruct((shorts + shorts // PACK, KVL), bf16),
+        ],
         scratch_shapes=[
             pltpu.VMEM((tokens, model), bf16),
             pltpu.VMEM((WIDTH, model), bf16),
             pltpu.VMEM((WIDTH, tokens), f32),
             pltpu.SMEM(lengths.shape, lengths.dtype),
-            pltpu.SMEM(owners.shape, owners.dtype),
             pltpu.VMEM(attn_gain.shape, bf16),
             pltpu.VMEM(kv_gain.shape, bf16),
-            pltpu.SemaphoreType.DMA((4,)),
+            pltpu.SemaphoreType.DMA((3,)),
             pltpu.SemaphoreType.DMA((2, len(chunks))),
         ],
-        compiler_params=pltpu.CompilerParams(vmem_limit_bytes=60 * 1024 * 1024),
+        compiler_params=params(),
         cost_estimate=pl.CostEstimate(
             flops=2 * tokens * model * WIDTH, bytes_accessed=2 * model * (tokens + WIDTH), transcendentals=0
         ),
         name="compress",
-    )(lengths, owners, hidden, attn_gain, w_dkv.T, kv_gain)
+    )(*[pltpu.with_memory_space_constraint(v, pltpu.HBM) for v in (lengths, hidden, attn_gain, w_dkv.T, kv_gain)])
 
     long_rows, short_rows = zs * xs * steps * local, zs * (count - 1) * steps * local
-    long_q, short_q = pl.pallas_call(
+    long_q, short_q, mask, order = pl.pallas_call(
         functools.partial(pick_kernel, most, sizes),
         in_specs=[SMEM, SMEM, HBM],
-        out_specs=[VMEM, VMEM],
-        out_shape=[jax.ShapeDtypeStruct((long_rows, WIDTH), bf16), jax.ShapeDtypeStruct((short_rows, WIDTH), bf16)],
+        out_specs=[VMEM] * 4,
+        out_shape=[
+            jax.ShapeDtypeStruct((long_rows, WIDTH), bf16),
+            jax.ShapeDtypeStruct((short_rows, WIDTH), bf16),
+            jax.ShapeDtypeStruct((short_rows // zs, shorts), f32),
+            jax.ShapeDtypeStruct((2 * count, 128), f32),
+        ],
         scratch_shapes=[
             pltpu.VMEM((count, steps, WIDTH, heads), bf16),
             pltpu.VMEM((long_rows, WIDTH), f32),
@@ -432,11 +464,12 @@
         name="pick_queries",
     )(lengths, owners, queries.transpose(0, 1, 3, 2))
 
-    short_in = [short_keys] + [send(short_keys, dx=j) for j in range(1, xs)]
-    long_in = [long_keys] + [send(long_keys, dc=j) for j in range(1, cores)]
+    short_in = [send(short_keys, by_x=j) for j in range(1, xs)]
+    row_in = [row_keys] + [send(row_keys, by_core=j) for j in range(1, cores)]
+
     x_rows = long_rows // xs + STAT_ROWS
     parts = pl.pallas_call(
-        lambda q, *refs: long_kernel(q, refs[:cores], refs[cores:]),
+        lambda q, *refs: long_kernel(most, q, refs[:cores], refs[cores:]),
         in_specs=[VMEM] * (1 + cores),
         out_specs=[VMEM] * xs,
         out_shape=[jax.ShapeDtypeStruct((x_rows, KVL), bf16)] * xs,
@@ -445,29 +478,26 @@
             flops=2 * long_rows * most * cores * (WIDTH + KVL), bytes_accessed=4 * most * WIDTH, transcendentals=0
         ),
         name="long_part",
-    )(long_q, *long_in)
-    sent = [send(parts[j], dx=j) for j in range(1, xs)]
+    )(long_q, *row_in)
+    sent = [send(parts[j], by_x=j) for j in range(1, xs)]
     own, *short_in = lax.optimization_barrier((parts[0], *short_in))
     parts = [own] + sent
-    short_in = short_in + [send(k, dc=j) for j in range(1, cores) for k in short_in]
+    short_in = short_in + [send(k, by_core=j) for j in range(1, cores) for k in short_in]
 
     per_short, per_long = short_rows // zs, long_rows // xs // zs
+    ins = cores + len(short_in)
     *short_parts, short_lse = pl.pallas_call(
-        lambda a, b, q, *refs: short_kernel(
-            most, a, b, q, refs[: len(short_in)], refs[len(short_in) : len(short_in) + zs], refs[-1]
-        ),
-        in_specs=[SMEM, SMEM] + [VMEM] * (1 + len(short_in)),
+        lambda q, m, *refs: short_kernel(most, q, m, refs[:cores], refs[cores:ins], refs[ins : ins + zs], refs[-1]),
+        in_specs=[VMEM] * (2 + ins),
         out_specs=[VMEM] * (zs + 1),
         out_shape=[jax.ShapeDtypeStruct((per_short, KVL), bf16)] * zs + [jax.ShapeDtypeStruct((zs, 8, per_short), f32)],
         compiler_params=params(),
         cost_estimate=pl.CostEstimate(
-            flops=2 * short_rows * shorts * len(short_in) * (WIDTH + KVL),
-            bytes_accessed=4 * shorts * len(short_in) * WIDTH,
-            transcendentals=0,
+            flops=2 * short_rows * shorts * ins * (WIDTH + KVL), bytes_accessed=4 * shorts * ins * WIDTH, transcendentals=0
         ),
         name="short_part",
-    )(lengths, owners, short_q, *short_in)
-    short_parts = [short_parts[0]] + [send(short_parts[k], dz=k) for k in range(1, zs)]
+    )(short_q, mask, *row_in, *short_in)
+    short_parts = [short_parts[0]] + [send(short_parts[k], by_z=k) for k in range(1, zs)]
 
     long_parts = pl.pallas_call(
         lambda *refs: merge_kernel(refs[:xs], refs[xs], refs[xs + 1 :]),
@@ -478,8 +508,7 @@
         cost_estimate=pl.CostEstimate(flops=0, bytes_accessed=2 * xs * x_rows * KVL, transcendentals=0),
         name="long_merge",
     )(*parts, short_lse)
-    after = long_parts[0]
-    long_parts = [after] + [send(long_parts[k], dz=k) for k in range(1, zs)]
+    after = short_parts[1] if zs > 1 else long_parts[0]
 
     rows = per_short + per_long
     step_part, step_lse = pl.pallas_call(
@@ -492,15 +521,19 @@
         name="step_part",
     )(lengths, owners, long_q, short_q, step_rows, after)
 
+    step_part, *late = lax.optimization_barrier((step_part, *long_parts[3:]))
+    long_parts = [*long_parts[:3], *late]
+    long_parts = [long_parts[0]] + [send(long_parts[k], by_z=k) for k in range(1, zs)]
+
     out = pl.pallas_call(
-        lambda a, b, s, l, *refs: last_kernel(most, a, b, s, l, refs[:zs], refs[zs : 2 * zs], refs[2 * zs]),
-        in_specs=[SMEM, SMEM] + [VMEM] * (2 + 2 * zs),
+        lambda o, s, l, *refs: last_kernel(o, s, l, refs[:zs], refs[zs : 2 * zs], refs[2 * zs]),
+        in_specs=[VMEM] * (3 + 2 * zs),
         out_specs=VMEM,
         out_shape=jax.ShapeDtypeStruct((count, steps * local, KVL), bf16),
         compiler_params=params(),
         cost_estimate=pl.CostEstimate(flops=0, bytes_accessed=2 * zs * rows * KVL, transcendentals=0),
         name="combine",
-    )(lengths, owners, step_part, step_lse, *short_parts, *long_parts)
+    )(order, step_part, step_lse, *short_parts, *long_parts)
     return out.reshape(count, steps, local, KVL)
 
 

time: 43.5 us -> 35.8 us (0.82)
  Pallas kernels: 20.2 us -> 15 us
  waiting for transfers between devices: 9.06 us -> 6.17 us
  starting transfers between devices: 12 us -> 14.4 us
  local copies, waits for them, and re-layouts: 1.95 us -> 0.01 us
    pallas_call x1, Pallas kernels: 12.6 us -> 8.6 us  [shards(): pl.pallas_call(functools.partial(compress_kernel, most, chunks), in_specs...]
    ppermute x11 -> x10, waiting for transfers between devices: 9.06 us -> 6.17 us  [send(): return lax.ppermute(value, 'ctx', pairs)]
    ppermute x11 -> x10, starting transfers between devices: 12 us -> 14.4 us  [send(): return lax.ppermute(value, 'ctx', pairs)]
    unnamed x12 -> x8, local copies, waits for them, and re-layouts: 1.95 us -> 0.01 us
    pallas_call x3, Pallas kernels: 4.02 us -> 2.82 us  [the longest x1 1.01 us: shards(): pl.pallas_call(lambda q, *refs: long_kernel(most, q, refs[:cores], refs[c...]
  transfers between devices with their start and end apart: 11 -> 10, of which waited for: 4 -> 3; matrix products, arithmetic and copies ran while one was open for 0% -> 0% of each run, Pallas kernels for 14% -> 15%
where the time goes in v2:
time: 35.8 us; the launch traced here: 35.6 us
  Pallas kernels  15 us (42%)
  starting transfers between devices  14.4 us (40%)
  waiting for transfers between devices  6.17 us (17%)
    ppermute x10, starting transfers between devices, send(): return lax.ppermute(value, 'ctx', pairs)  14.4 us
    pallas_call x1, Pallas kernels, shards(): pl.pallas_call(functools.partial(compress_kernel, most, chunks), in_specs...  8.6 us
    ppermute x10, waiting for transfers between devices, send(): return lax.ppermute(value, 'ctx', pairs)  6.17 us
    pallas_call x1, Pallas kernels, shards(): pl.pallas_call(functools.partial(pick_kernel, most, sizes), in_specs=[SME...  2.42 us
    pallas_call x1, Pallas kernels, shards(): pl.pallas_call(functools.partial(step_kernel, most, steps), in_specs=[SME...  1.02 us
    pallas_call x1, Pallas kernels, shards(): pl.pallas_call(lambda q, *refs: long_kernel(most, q, refs[:cores], refs[c...  1.01 us
    pallas_call x1, Pallas kernels, shards(): pl.pallas_call(lambda o, s, l, *refs: last_kernel(o, s, l, refs[:zs], ref...  0.91 us
    pallas_call x1, Pallas kernels, shards(): pl.pallas_call(lambda q, m, *refs: short_kernel(most, q, m, refs[:cores],...  0.9 us
  transfers between devices with their start and end apart: 10, of which 3 were waited for; matrix products, arithmetic and copies ran while one was open for 0% of the time, Pallas kernels for 15%

profile of v2, /device:TPU:0, one launch (start us, length us, event | category | flops | bytes accessed | tf_op | source)
XLA Modules:
  0.0 35.6 jit_solution(2054979885542824884)
XLA Ops:
  0.0 0.0 copy-start
  0.0 0.0 copy-start.2
  0.0 0.0 copy-start.3
  0.0 0.0 copy-start.1
  0.0 8.6 %compress.1 = (bf16[576,512]{1,0:T(8,128)(2,1)S(1)}, bf16[144,512]{1,0:T(8,128)(2,1)S(1)}) custom-call(s32[4]{0:T(128)} %lengths_ref.3, bf16[512,7168]{1,0:T(8,128)(2,1)} %x_hbm.1, bf16[7168]{0:T(1024)(128)(2,1)} %gain_hbm.1, bf16[576,7168]{1,0:T(8,128)(2,1)} %bitcast.4, bf16[512]{0:T(512)(128)(2,1)} %kv_gain_hbm.1), custom_call_target="tpu_custom_call" | custom-call | flops 4227858432 | bytes 15597568 | tf_op jit(solution)/shard_map/compress/pallas_call | solution.py:416
  8.6 0.5 %collective-permute-start = (bf16[576,512]{1,0:T(8,128)(2,1)S(1)}, bf16[576,512]{1,0:T(8,128)(2,1)S(1)}, u32[]{:S(2)}, u32[]{:S(2)}) collective-permute-start(bf16[576,512]{1,0:T(8,128)(2,1)S(1)} %get-tuple-element.32.refs_0_), channel_id=1, source_target_pairs={{0,1},{1,0},{2,3},{3,2},{4,5},{5,4},{6,7},{7,6},{8,9},{9,8},{10,11... | collective-permute-start | bytes 1769480 | tf_op jit(solution)/shard_map/ppermute | solution.py:411
  9.1 2.6 %collective-permute-start.1 = (bf16[144,512]{1,0:T(8,128)(2,1)S(1)}, bf16[144,512]{1,0:T(8,128)(2,1)S(1)}, u32[]{:S(2)}, u32[]{:S(2)}) collective-permute-start(bf16[144,512]{1,0:T(8,128)(2,1)S(1)} %get-tuple-element.34), channel_id=1, source_target_pairs={{0,2},{1,3},{2,0},{3,1},{4,6},{5,7},{6,4},{7,5},{8,10},{9,11},{10,... | collective-permute-start | bytes 442376 | tf_op jit(solution)/shard_map/ppermute | solution.py:411
  11.7 0.0 copy-done
  11.7 0.0 copy-done.2
  11.7 0.0 copy-done.3
  11.7 2.4 %pick_queries.1 = (bf16[256,576]{1,0:T(8,128)(2,1)S(1)}, bf16[384,576]{1,0:T(8,128)(2,1)S(1)}, f32[96,128]{1,0:T(8,128)S(1)}, f32[8,128]{1,0:T(8,128)S(1)}) custom-call(s32[4]{0:T(128)S(1)} %copy-done.2, s32[4]{0:T(128)S(1)} %copy-done.3, bf16[4,4,576,128]{3,2,1,0:T(8,128)(2,1)S(1)} %bitcast.3), custom_call_target="tpu_custom_call" | custom-call | flops 94371840 | bytes 2359296 | tf_op jit(solution)/shard_map/pick_queries/pallas_call | solution.py:442
  14.1 0.0 collective-permute-done.refs_1_
  14.1 1.0 %long_part.1 = (bf16[136,512]{1,0:T(8,128)(2,1)S(1)}, bf16[136,512]{1,0:T(8,128)(2,1)S(1)}) custom-call(bf16[256,576]{1,0:T(8,128)(2,1)S(1)} %get-tuple-element.29.q.long_q_ref, bf16[576,512]{1,0:T(8,128)(2,1)S(1)} %get-tuple-element.32.refs_0_, bf16[576,512]{1,0:T(8,128)(2,1)S(1)} %collective-permute-done.refs_1_), custom_call_target="tpu_custom_call" | custom-call | flops 427819008 | bytes 884736 | tf_op jit(solution)/shard_map/long_part/pallas_call | solution.py:471
  15.1 1.0 %collective-permute-done.1.refs_2_ = bf16[144,512]{1,0:T(8,128)(2,1)S(1)} collective-permute-done((bf16[144,512]{1,0:T(8,128)(2,1)S(1)}, bf16[144,512]{1,0:T(8,128)(2,1)S(1)}, u32[]{:S(2)}, u32[]{:S(2)}) %collective-permute-start.1) | collective-permute-done | bytes 147488 | tf_op jit(solution)/shard_map/ppermute | solution.py:411
  16.1 0.0 collective-permute-start.2
  16.1 1.8 %collective-permute-start.4 = (bf16[136,512]{1,0:T(8,128)(2,1)S(1)}, bf16[136,512]{1,0:T(8,128)(2,1)S(1)}, u32[]{:S(2)}, u32[]{:S(2)}) collective-permute-start(bf16[136,512]{1,0:T(8,128)(2,1)S(1)} %get-tuple-element.39), channel_id=1, source_target_pairs={{0,2},{1,3},{2,0},{3,1},{4,6},{5,7},{6,4},{7,5},{8,10},{9,11},{10,... | collective-permute-start | bytes 417800 | tf_op jit(solution)/shard_map/ppermute | solution.py:411
  17.9 0.0 collective-permute-done.2.refs_3_
  17.9 0.9 %short_part.1 = (bf16[96,512]{1,0:T(8,128)(2,1)S(1)}, bf16[96,512]{1,0:T(8,128)(2,1)S(1)}, bf16[96,512]{1,0:T(8,128)(2,1)S(1)}, bf16[96,512]{1,0:T(8,128)(2,1)S(1)}, f32[4,8,96]{2,1,0:T(8,128)S(1)}) custom-call(bf16[384,576]{1,0:T(8,128)(2,1)S(1)} %get-tuple-element.30.q.short_q_ref, f32[96,128]{1,0:T(8,128)S(1)} %get-tuple-element.31.m, ...), custom_call_target="tpu_custom_call" | custom-call | flops 427819008 | bytes 1179648 | tf_op jit(solution)/shard_map/short_part/pallas_call | solution.py:489
  18.8 1.6 %collective-permute-start.3 = (bf16[96,512]{1,0:T(8,128)(2,1)S(1)}, bf16[96,512]{1,0:T(8,128)(2,1)S(1)}, u32[]{:S(2)}, u32[]{:S(2)}) collective-permute-start(bf16[96,512]{1,0:T(8,128)(2,1)S(1)} %get-tuple-element.36), channel_id=1, source_target_pairs={{0,4},{1,5},{2,6},{3,7},{4,8},{5,9},{6,10},{7,11},{8,12},{9,13},{1... | collective-permute-start | bytes 294920 | tf_op jit(solution)/shard_map/ppermute | solution.py:411
  20.4 2.6 %collective-permute-start.5 = (bf16[96,512]{1,0:T(8,128)(2,1)S(1)}, bf16[96,512]{1,0:T(8,128)(2,1)S(1)}, u32[]{:S(2)}, u32[]{:S(2)}) collective-permute-start(bf16[96,512]{1,0:T(8,128)(2,1)S(1)} %get-tuple-element.45), channel_id=1, source_target_pairs={{0,8},{1,9},{2,10},{3,11},{4,12},{5,13},{6,14},{7,15},{8,0},{9,1},... | collective-permute-start | bytes 294920 | tf_op jit(solution)/shard_map/ppermute | solution.py:411
  23.0 1.4 %collective-permute-start.6 = (bf16[96,512]{1,0:T(8,128)(2,1)S(1)}, bf16[96,512]{1,0:T(8,128)(2,1)S(1)}, u32[]{:S(2)}, u32[]{:S(2)}) collective-permute-start(bf16[96,512]{1,0:T(8,128)(2,1)S(1)} %get-tuple-element.46), channel_id=1, source_target_pairs={{0,12},{1,13},{2,14},{3,15},{4,0},{5,1},{6,2},{7,3},{8,4},{9,5},{1... | collective-permute-start | bytes 294920 | tf_op jit(solution)/shard_map/ppermute | solution.py:411
  24.4 0.0 collective-permute-done.4.refs_1_
  24.4 0.2 long_merge.1
  24.6 0.7 %collective-permute-start.7 = (bf16[40,512]{1,0:T(8,128)(2,1)S(1)}, bf16[40,512]{1,0:T(8,128)(2,1)S(1)}, u32[]{:S(2)}, u32[]{:S(2)}) collective-permute-start(bf16[40,512]{1,0:T(8,128)(2,1)S(1)} %get-tuple-element.48), channel_id=1, source_target_pairs={{0,4},{1,5},{2,6},{3,7},{4,8},{5,9},{6,10},{7,11},{8,12},{9,13},{1... | collective-permute-start | bytes 122888 | tf_op jit(solution)/shard_map/ppermute | solution.py:411
  25.3 1.6 %collective-permute-start.8 = (bf16[40,512]{1,0:T(8,128)(2,1)S(1)}, bf16[40,512]{1,0:T(8,128)(2,1)S(1)}, u32[]{:S(2)}, u32[]{:S(2)}) collective-permute-start(bf16[40,512]{1,0:T(8,128)(2,1)S(1)} %get-tuple-element.49), channel_id=1, source_target_pairs={{0,8},{1,9},{2,10},{3,11},{4,12},{5,13},{6,14},{7,15},{8,0},{9,1},... | collective-permute-start | bytes 122888 | tf_op jit(solution)/shard_map/ppermute | solution.py:411
  26.9 0.0 collective-permute-done.3.after_ref.refs_1_
  26.9 0.0 copy-done.1
  26.9 1.0 %step_part.1 = (f32[128,512]{1,0:T(8,128)S(1)}, f32[8,128]{1,0:T(8,128)S(1)}) custom-call(s32[4]{0:T(128)S(1)} %copy-done.2, s32[4]{0:T(128)S(1)} %copy-done.3, bf16[256,576]{1,0:T(8,128)(2,1)S(1)} %get-tuple-element.29.q.long_q_ref, bf16[384,576]{1,0:T(8,128)(2,1)S(1)} %get-tuple-element.30.q.short_q_ref, bf16[4,4,576]{2,1,0:T(4,128)(2,1)S(1)} %copy-done.1, ...), custom_call_target="tpu_custom_call" | custom-call | bytes 262144 | tf_op jit(solution)/shard_map/step_part/pallas_call | solution.py:514
  27.9 1.6 %collective-permute-start.9 = (bf16[40,512]{1,0:T(8,128)(2,1)S(1)}, bf16[40,512]{1,0:T(8,128)(2,1)S(1)}, u32[]{:S(2)}, u32[]{:S(2)}) collective-permute-start(bf16[40,512]{1,0:T(8,128)(2,1)S(1)} %get-tuple-element.50), channel_id=1, source_target_pairs={{0,12},{1,13},{2,14},{3,15},{4,0},{5,1},{6,2},{7,3},{8,4},{9,5},{1... | collective-permute-start | bytes 122888 | tf_op jit(solution)/shard_map/ppermute | solution.py:411
  29.5 1.9 %collective-permute-done.7.refs_5_ = bf16[40,512]{1,0:T(8,128)(2,1)S(1)} collective-permute-done((bf16[40,512]{1,0:T(8,128)(2,1)S(1)}, bf16[40,512]{1,0:T(8,128)(2,1)S(1)}, u32[]{:S(2)}, u32[]{:S(2)}) %collective-permute-start.7) | collective-permute-done | bytes 40992 | tf_op jit(solution)/shard_map/ppermute | solution.py:411
  31.4 3.3 %collective-permute-done.8.refs_6_ = bf16[40,512]{1,0:T(8,128)(2,1)S(1)} collective-permute-done((bf16[40,512]{1,0:T(8,128)(2,1)S(1)}, bf16[40,512]{1,0:T(8,128)(2,1)S(1)}, u32[]{:S(2)}, u32[]{:S(2)}) %collective-permute-start.8) | collective-permute-done | bytes 40992 | tf_op jit(solution)/shard_map/ppermute | solution.py:411
  34.7 0.0 collective-permute-done.5.refs_2_
  34.7 0.0 collective-permute-done.6.refs_3_
  34.7 0.0 collective-permute-done.9.refs_7_
  34.7 0.9 %combine.1 = bf16[4,32,512]{2,1,0:T(8,128)(2,1)} custom-call(f32[8,128]{1,0:T(8,128)S(1)} %get-tuple-element.28.o, f32[128,512]{1,0:T(8,128)S(1)} %get-tuple-element.42.s, f32[8,128]{1,0:T(8,128)S(1)} %get-tuple-element.43.l, bf16[96,512]{1,0:T(8,128)(2,1)S(1)} %get-tuple-element.44.refs_0_, bf16[96,512]{1,0:T(8,128)(2,1)S(1)} %collective-permute-done.3.after_ref.refs_1_, ...), custom_call_target="tpu_custom_call" | custom-call | bytes 524288 | tf_op jit(solution)/shard_map/combine/pallas_call | solution.py:528
Async XLA Ops:
  0.0 11.7 %copy-start = (bf16[4,4,128,576]{2,3,1,0:T(8,128)(2,1)S(1)}, bf16[4,4,128,576]{2,3,1,0:T(8,128)(2,1)}, u32[]{:S(2)}) copy-start(bf16[4,4,128,576]{2,3,1,0:T(8,128)(2,1)} %param.14) | copy-start | bytes 7077892
  0.0 11.7 %copy-start.2 = (s32[4]{0:T(128)S(1)}, s32[4]{0:T(128)}, u32[]{:S(2)}) copy-start(s32[4]{0:T(128)} %lengths_ref.3) | copy-start | bytes 52
  0.0 11.7 %copy-start.3 = (s32[4]{0:T(128)S(1)}, s32[4]{0:T(128)}, u32[]{:S(2)}) copy-start(s32[4]{0:T(128)} %owners_ref.3) | copy-start | bytes 52
  0.0 26.9 %copy-start.1 = (bf16[4,4,576]{2,1,0:T(4,128)(2,1)S(1)}, bf16[4,4,576]{2,1,0:T(4,128)(2,1)}, u32[]{:S(2)}) copy-start(bf16[4,4,576]{2,1,0:T(4,128)(2,1)} %step_ref.1) | copy-start | bytes 55300
  8.6 5.5 %collective-permute-start = (bf16[576,512]{1,0:T(8,128)(2,1)S(1)}, bf16[576,512]{1,0:T(8,128)(2,1)S(1)}, u32[]{:S(2)}, u32[]{:S(2)}) collective-permute-start(bf16[576,512]{1,0:T(8,128)(2,1)S(1)} %get-tuple-element.32.refs_0_), channel_id=1, source_target_pairs={{0,1},{1,0},{2,3},{3,2},{4,5},{5,4},{6,7},{7,6},{8,9},{9,8},{10,11... | collective-permute-start | bytes 1769480 | tf_op jit(solution)/shard_map/ppermute | solution.py:411
  9.1 7.0 %collective-permute-start.1 = (bf16[144,512]{1,0:T(8,128)(2,1)S(1)}, bf16[144,512]{1,0:T(8,128)(2,1)S(1)}, u32[]{:S(2)}, u32[]{:S(2)}) collective-permute-start(bf16[144,512]{1,0:T(8,128)(2,1)S(1)} %get-tuple-element.34), channel_id=1, source_target_pairs={{0,2},{1,3},{2,0},{3,1},{4,6},{5,7},{6,4},{7,5},{8,10},{9,11},{10,... | collective-permute-start | bytes 442376 | tf_op jit(solution)/shard_map/ppermute | solution.py:411
  16.1 1.8 %collective-permute-start.2 = (bf16[144,512]{1,0:T(8,128)(2,1)S(1)}, bf16[144,512]{1,0:T(8,128)(2,1)S(1)}, u32[]{:S(2)}, u32[]{:S(2)}) collective-permute-start(bf16[144,512]{1,0:T(8,128)(2,1)S(1)} %collective-permute-done.1.refs_2_), channel_id=1, source_target_pairs={{0,1},{1,0},{2,3},{3,2},{4,5},{5,4},{6,7},{7,6},{8,9},{9,8},{10,11... | collective-permute-start | bytes 442376 | tf_op jit(solution)/shard_map/ppermute | solution.py:411
  16.1 8.3 %collective-permute-start.4 = (bf16[136,512]{1,0:T(8,128)(2,1)S(1)}, bf16[136,512]{1,0:T(8,128)(2,1)S(1)}, u32[]{:S(2)}, u32[]{:S(2)}) collective-permute-start(bf16[136,512]{1,0:T(8,128)(2,1)S(1)} %get-tuple-element.39), channel_id=1, source_target_pairs={{0,2},{1,3},{2,0},{3,1},{4,6},{5,7},{6,4},{7,5},{8,10},{9,11},{10,... | collective-permute-start | bytes 417800 | tf_op jit(solution)/shard_map/ppermute | solution.py:411
  18.8 8.1 %collective-permute-start.3 = (bf16[96,512]{1,0:T(8,128)(2,1)S(1)}, bf16[96,512]{1,0:T(8,128)(2,1)S(1)}, u32[]{:S(2)}, u32[]{:S(2)}) collective-permute-start(bf16[96,512]{1,0:T(8,128)(2,1)S(1)} %get-tuple-element.36), channel_id=1, source_target_pairs={{0,4},{1,5},{2,6},{3,7},{4,8},{5,9},{6,10},{7,11},{8,12},{9,13},{1... | collective-permute-start | bytes 294920 | tf_op jit(solution)/shard_map/ppermute | solution.py:411
  20.4 14.3 %collective-permute-start.5 = (bf16[96,512]{1,0:T(8,128)(2,1)S(1)}, bf16[96,512]{1,0:T(8,128)(2,1)S(1)}, u32[]{:S(2)}, u32[]{:S(2)}) collective-permute-start(bf16[96,512]{1,0:T(8,128)(2,1)S(1)} %get-tuple-element.45), channel_id=1, source_target_pairs={{0,8},{1,9},{2,10},{3,11},{4,12},{5,13},{6,14},{7,15},{8,0},{9,1},... | collective-permute-start | bytes 294920 | tf_op jit(solution)/shard_map/ppermute | solution.py:411
  23.0 11.7 %collective-permute-start.6 = (bf16[96,512]{1,0:T(8,128)(2,1)S(1)}, bf16[96,512]{1,0:T(8,128)(2,1)S(1)}, u32[]{:S(2)}, u32[]{:S(2)}) collective-permute-start(bf16[96,512]{1,0:T(8,128)(2,1)S(1)} %get-tuple-element.46), channel_id=1, source_target_pairs={{0,12},{1,13},{2,14},{3,15},{4,0},{5,1},{6,2},{7,3},{8,4},{9,5},{1... | collective-permute-start | bytes 294920 | tf_op jit(solution)/shard_map/ppermute | solution.py:411
  24.6 6.8 %collective-permute-start.7 = (bf16[40,512]{1,0:T(8,128)(2,1)S(1)}, bf16[40,512]{1,0:T(8,128)(2,1)S(1)}, u32[]{:S(2)}, u32[]{:S(2)}) collective-permute-start(bf16[40,512]{1,0:T(8,128)(2,1)S(1)} %get-tuple-element.48), channel_id=1, source_target_pairs={{0,4},{1,5},{2,6},{3,7},{4,8},{5,9},{6,10},{7,11},{8,12},{9,13},{1... | collective-permute-start | bytes 122888 | tf_op jit(solution)/shard_map/ppermute | solution.py:411
  25.3 9.4 %collective-permute-start.8 = (bf16[40,512]{1,0:T(8,128)(2,1)S(1)}, bf16[40,512]{1,0:T(8,128)(2,1)S(1)}, u32[]{:S(2)}, u32[]{:S(2)}) collective-permute-start(bf16[40,512]{1,0:T(8,128)(2,1)S(1)} %get-tuple-element.49), channel_id=1, source_target_pairs={{0,8},{1,9},{2,10},{3,11},{4,12},{5,13},{6,14},{7,15},{8,0},{9,1},... | collective-permute-start | bytes 122888 | tf_op jit(solution)/shard_map/ppermute | solution.py:411
  27.9 6.8 %collective-permute-start.9 = (bf16[40,512]{1,0:T(8,128)(2,1)S(1)}, bf16[40,512]{1,0:T(8,128)(2,1)S(1)}, u32[]{:S(2)}, u32[]{:S(2)}) collective-permute-start(bf16[40,512]{1,0:T(8,128)(2,1)S(1)} %get-tuple-element.50), channel_id=1, source_target_pairs={{0,12},{1,13},{2,14},{3,15},{4,0},{5,1},{6,2},{7,3},{8,4},{9,5},{1... | collective-permute-start | bytes 122888 | tf_op jit(solution)/shard_map/ppermute | solution.py:411

commit v3 on v2

--- a/solution.py
+++ b/solution.py
@@ -27,6 +27,12 @@
     chips = devices // cores
     along_x = max(k for k in range(1, chips + 1) if chips % k == 0 and k * k * k <= chips)
     return chips // along_x, along_x, cores
+
+
+def shifted(z, by, zs):
+    if zs & (zs - 1) == 0:
+        return z ^ by
+    return (z + by) % zs
 
 
 def scalars(lengths_ref, owners_ref, most):
@@ -214,7 +220,7 @@
     def head_of(rows, spread):
         row = lax.broadcasted_iota(jnp.int32, (rows, heads), 0)
         unit, inner = row // local, lax.rem(row, local)
-        z = lax.rem(lax.rem(unit, zs) + here_z, zs)
+        z = shifted(here_z, lax.rem(unit, zs), zs)
         x = lax.rem(unit // zs + here_x, xs) if spread else here_x
         head = ((z * xs + x) * cores + core) * local + inner
         return (head == lax.broadcasted_iota(jnp.int32, (rows, heads), 1)).astype(jnp.bfloat16)
@@ -332,7 +338,9 @@
         ref[...] = jnp.concatenate([mixed[part], stat_rows(both)], axis=0).astype(jnp.bfloat16)
 
 
-def step_kernel(most, steps, lengths_ref, owners_ref, long_q_ref, short_q_ref, step_ref, after_ref, out_ref, lse_ref):
+def step_kernel(
+    most, steps, lengths_ref, owners_ref, long_q_ref, short_q_ref, step_ref, short_ref, long_ref, out_ref, lse_ref
+):
     count = lengths_ref.shape[0]
     _, _, long_block = scalars(lengths_ref, owners_ref, most)
     blocks = [jnp.where(long_block <= i, i + 1, i) for i in range(count - 1)] + [long_block]
@@ -351,13 +359,22 @@
     peak = jnp.max(scores, axis=1, keepdims=True)
     weights = jnp.where(allowed, jnp.exp(scores - peak), 0.0)
     total = jnp.sum(weights, axis=1, keepdims=True)
-    out_ref[...] = jnp.dot(weights.astype(jnp.bfloat16), keys[:, :KVL], preferred_element_type=jnp.float32) / total
-    lse_ref[...] = as_line(peak + jnp.log(total))
+    mixed = jnp.dot(weights.astype(jnp.bfloat16), keys[:, :KVL], preferred_element_type=jnp.float32) / total
+    line = as_line(peak + jnp.log(total))[:1]
+    long = long_ref[...].astype(jnp.float32)
+    own = jnp.concatenate([short_ref[...].astype(jnp.float32), long[:per_slot]], axis=0)
+    own_line = read_line(long[per_slot:], rows)
+    top = jnp.maximum(line, own_line)
+    share, own_share = jnp.exp(line - top), jnp.exp(own_line - top)
+    whole = share + own_share
+    out_ref[...] = wide(as_columns(share / whole)) * mixed + wide(as_columns(own_share / whole)) * own
+    lse_ref[...] = jnp.broadcast_to(top + jnp.log(whole), lse_ref.shape)
 
 
 def last_kernel(order_ref, step_ref, step_lse_ref, short_refs, long_refs, out_ref):
     count = out_ref.shape[0]
-    rows, per_slot = step_ref.shape[0], long_refs[0].shape[0] - STAT_ROWS
+    rows = step_ref.shape[0]
+    per_slot = rows // count
     shorts = rows - per_slot
     longs = [ref[...].astype(jnp.float32) for ref in long_refs]
     lines = [step_lse_ref[:1]] + [read_line(part[per_slot:], rows) for part in longs]
@@ -400,19 +417,19 @@
 
     def send(value, by_z=0, by_x=0, by_core=0):
         def device(z, x, c):
-            return (z % zs * xs + x % xs) * cores + c % cores
+            return (z * xs + x % xs) * cores + c % cores
 
         pairs = [
-            (device(z, x, c), device(z + by_z, x + by_x, c + by_core))
+            (device(z, x, c), device(shifted(z, by_z, zs), x + by_x, c + by_core))
             for z in range(zs)
             for x in range(xs)
             for c in range(cores)
         ]
         return lax.ppermute(value, "ctx", pairs)
 
-    chunks = [1024] * ((model - 1024) // 1024)
-    while sum(chunks) < model:
-        chunks.append(min(512, model - sum(chunks)))
+    chunks = [1024] * (model // 1024)
+    if sum(chunks) < model:
+        chunks.append(model - sum(chunks))
     row_keys, short_keys = pl.pallas_call(
         functools.partial(compress_kernel, most, chunks),
         in_specs=[HBM] * 5,
@@ -462,7 +479,7 @@
             transcendentals=0,
         ),
         name="pick_queries",
-    )(lengths, owners, queries.transpose(0, 1, 3, 2))
+    )(lengths, owners, pltpu.with_memory_space_constraint(queries.transpose(0, 1, 3, 2), pltpu.HBM))
 
     short_in = [send(short_keys, by_x=j) for j in range(1, xs)]
     row_in = [row_keys] + [send(row_keys, by_core=j) for j in range(1, cores)]
@@ -497,7 +514,9 @@
         ),
         name="short_part",
     )(short_q, mask, *row_in, *short_in)
-    short_parts = [short_parts[0]] + [send(short_parts[k], by_z=k) for k in range(1, zs)]
+    turns = [*range(2, zs), 1] if zs > 1 else []
+    came = {k: send(short_parts[k], by_z=k) for k in turns}
+    short_parts = [came.get(k, part) for k, part in enumerate(short_parts)]
 
     long_parts = pl.pallas_call(
         lambda *refs: merge_kernel(refs[:xs], refs[xs], refs[xs + 1 :]),
@@ -508,32 +527,35 @@
         cost_estimate=pl.CostEstimate(flops=0, bytes_accessed=2 * xs * x_rows * KVL, transcendentals=0),
         name="long_merge",
     )(*parts, short_lse)
-    after = short_parts[1] if zs > 1 else long_parts[0]
 
     rows = per_short + per_long
     step_part, step_lse = pl.pallas_call(
         functools.partial(step_kernel, most, steps),
-        in_specs=[SMEM, SMEM, VMEM, VMEM, VMEM, HBM],
+        in_specs=[SMEM, SMEM] + [VMEM] * 5,
         out_specs=[VMEM, VMEM],
         out_shape=[jax.ShapeDtypeStruct((rows, KVL), f32), jax.ShapeDtypeStruct((8, rows), f32)],
         compiler_params=params(),
         cost_estimate=pl.CostEstimate(flops=0, bytes_accessed=4 * rows * KVL, transcendentals=0),
         name="step_part",
-    )(lengths, owners, long_q, short_q, step_rows, after)
-
-    step_part, *late = lax.optimization_barrier((step_part, *long_parts[3:]))
-    long_parts = [*long_parts[:3], *late]
-    long_parts = [long_parts[0]] + [send(long_parts[k], by_z=k) for k in range(1, zs)]
+    )(lengths, owners, long_q, short_q, step_rows, short_parts[0], long_parts[0])
+
+    late = turns[2:]
+    tied = [long_parts[k] for k in late]
+    if late:
+        short_parts[turns[0]], *tied = lax.optimization_barrier((short_parts[turns[0]], *tied))
+    ready = dict(zip(late, tied))
+    came = {k: send(ready.get(k, long_parts[k]), by_z=k) for k in turns}
+    long_parts = [came[k] for k in range(1, zs)]
 
     out = pl.pallas_call(
-        lambda o, s, l, *refs: last_kernel(o, s, l, refs[:zs], refs[zs : 2 * zs], refs[2 * zs]),
-        in_specs=[VMEM] * (3 + 2 * zs),
+        lambda o, s, l, *refs: last_kernel(o, s, l, refs[: zs - 1], refs[zs - 1 : -1], refs[-1]),
+        in_specs=[VMEM] * (1 + 2 * zs),
         out_specs=VMEM,
         out_shape=jax.ShapeDtypeStruct((count, steps * local, KVL), bf16),
         compiler_params=params(),
         cost_estimate=pl.CostEstimate(flops=0, bytes_accessed=2 * zs * rows * KVL, transcendentals=0),
         name="combine",
-    )(order, step_part, step_lse, *short_parts, *long_parts)
+    )(order, step_part, step_lse, *short_parts[1:], *long_parts)
     return out.reshape(count, steps, local, KVL)
 
 

time: 35.8 us -> 34.7 us (0.969)
  starting transfers between devices: 14.4 us -> 13.2 us
    ppermute x10, starting transfers between devices: 14.4 us -> 13.2 us  [send(): return lax.ppermute(value, 'ctx', pairs)]
    pallas_call x1, Pallas kernels: 2.42 us -> 2.94 us  [shards(): pl.pallas_call(functools.partial(pick_kernel, most, sizes), in_specs=[SME...]
    pallas_call x1, Pallas kernels: 8.6 us -> 8.19 us  [shards(): pl.pallas_call(functools.partial(compress_kernel, most, chunks), in_specs...]
  transfers between devices with their start and end apart: 10 -> 10, of which waited for: 3 -> 3; matrix products, arithmetic and copies ran while one was open for 0% -> 0% of each run, Pallas kernels for 15% -> 18%
where the time goes in v3:
time: 34.7 us; the launch traced here: 34.6 us
  Pallas kernels  15.2 us (44%)
  starting transfers between devices  13.2 us (38%)
  waiting for transfers between devices  6.09 us (18%)
    ppermute x10, starting transfers between devices, send(): return lax.ppermute(value, 'ctx', pairs)  13.2 us
    pallas_call x1, Pallas kernels, shards(): pl.pallas_call(functools.partial(compress_kernel, most, chunks), in_specs...  8.19 us
    ppermute x10, waiting for transfers between devices, send(): return lax.ppermute(value, 'ctx', pairs)  6.09 us
    pallas_call x1, Pallas kernels, shards(): pl.pallas_call(functools.partial(pick_kernel, most, sizes), in_specs=[SME...  2.94 us
    pallas_call x1, Pallas kernels, shards(): pl.pallas_call(functools.partial(step_kernel, most, steps), in_specs=[SME...  1.11 us
    pallas_call x1, Pallas kernels, shards(): pl.pallas_call(lambda q, *refs: long_kernel(most, q, refs[:cores], refs[c...  1 us
    pallas_call x1, Pallas kernels, shards(): pl.pallas_call(lambda q, m, *refs: short_kernel(most, q, m, refs[:cores],...  0.9 us
    pallas_call x1, Pallas kernels, shards(): pl.pallas_call(lambda o, s, l, *refs: last_kernel(o, s, l, refs[:zs - 1],...  0.87 us
  transfers between devices with their start and end apart: 10, of which 3 were waited for; matrix products, arithmetic and copies ran while one was open for 0% of the time, Pallas kernels for 18%

profile of v3, /device:TPU:0, one launch (start us, length us, event | category | flops | bytes accessed | tf_op | source)
XLA Modules:
  0.0 34.6 jit_solution(17860715246089238715)
XLA Ops:
  0.0 0.0 copy-start.1
  0.0 0.0 copy-start.2
  0.0 0.0 copy-start
  0.0 8.2 %compress.1 = (bf16[576,512]{1,0:T(8,128)(2,1)S(1)}, bf16[144,512]{1,0:T(8,128)(2,1)S(1)}) custom-call(s32[4]{0:T(128)} %lengths_ref.3, bf16[512,7168]{1,0:T(8,128)(2,1)} %x_hbm.1, bf16[7168]{0:T(1024)(128)(2,1)} %gain_hbm.1, bf16[576,7168]{1,0:T(8,128)(2,1)} %bitcast.4, bf16[512]{0:T(512)(128)(2,1)} %kv_gain_hbm.1), custom_call_target="tpu_custom_call" | custom-call | flops 4227858432 | bytes 15597568 | tf_op jit(solution)/shard_map/compress/pallas_call | solution.py:433
  8.2 0.5 %collective-permute-start = (bf16[576,512]{1,0:T(8,128)(2,1)S(1)}, bf16[576,512]{1,0:T(8,128)(2,1)S(1)}, u32[]{:S(2)}, u32[]{:S(2)}) collective-permute-start(bf16[576,512]{1,0:T(8,128)(2,1)S(1)} %get-tuple-element.32.refs_0_), channel_id=1, source_target_pairs={{0,1},{1,0},{2,3},{3,2},{4,5},{5,4},{6,7},{7,6},{8,9},{9,8},{10,11... | collective-permute-start | bytes 1769480 | tf_op jit(solution)/shard_map/ppermute | solution.py:428
  8.7 2.6 %collective-permute-start.1 = (bf16[144,512]{1,0:T(8,128)(2,1)S(1)}, bf16[144,512]{1,0:T(8,128)(2,1)S(1)}, u32[]{:S(2)}, u32[]{:S(2)}) collective-permute-start(bf16[144,512]{1,0:T(8,128)(2,1)S(1)} %get-tuple-element.34), channel_id=1, source_target_pairs={{0,2},{1,3},{2,0},{3,1},{4,6},{5,7},{6,4},{7,5},{8,10},{9,11},{10,... | collective-permute-start | bytes 442376 | tf_op jit(solution)/shard_map/ppermute | solution.py:428
  11.3 0.0 copy-done.1
  11.3 0.0 copy-done.2
  11.3 2.9 %pick_queries.1 = (bf16[256,576]{1,0:T(8,128)(2,1)S(1)}, bf16[384,576]{1,0:T(8,128)(2,1)S(1)}, f32[96,128]{1,0:T(8,128)S(1)}, f32[8,128]{1,0:T(8,128)S(1)}) custom-call(s32[4]{0:T(128)S(1)} %copy-done.1, s32[4]{0:T(128)S(1)} %copy-done.2, bf16[4,4,576,128]{3,2,1,0:T(8,128)(2,1)} %bitcast.3), custom_call_target="tpu_custom_call" | custom-call | flops 94371840 | bytes 2359296 | tf_op jit(solution)/shard_map/pick_queries/pallas_call | solution.py:459
  14.3 0.0 collective-permute-done.refs_1_
  14.3 1.0 %long_part.1 = (bf16[136,512]{1,0:T(8,128)(2,1)S(1)}, bf16[136,512]{1,0:T(8,128)(2,1)S(1)}) custom-call(bf16[256,576]{1,0:T(8,128)(2,1)S(1)} %get-tuple-element.29.q.long_q_ref, bf16[576,512]{1,0:T(8,128)(2,1)S(1)} %get-tuple-element.32.refs_0_, bf16[576,512]{1,0:T(8,128)(2,1)S(1)} %collective-permute-done.refs_1_), custom_call_target="tpu_custom_call" | custom-call | flops 427819008 | bytes 884736 | tf_op jit(solution)/shard_map/long_part/pallas_call | solution.py:488
  15.3 0.5 %collective-permute-done.1.refs_2_ = bf16[144,512]{1,0:T(8,128)(2,1)S(1)} collective-permute-done((bf16[144,512]{1,0:T(8,128)(2,1)S(1)}, bf16[144,512]{1,0:T(8,128)(2,1)S(1)}, u32[]{:S(2)}, u32[]{:S(2)}) %collective-permute-start.1) | collective-permute-done | bytes 147488 | tf_op jit(solution)/shard_map/ppermute | solution.py:428
  15.7 0.0 collective-permute-start.2
  15.7 1.8 %collective-permute-start.3 = (bf16[136,512]{1,0:T(8,128)(2,1)S(1)}, bf16[136,512]{1,0:T(8,128)(2,1)S(1)}, u32[]{:S(2)}, u32[]{:S(2)}) collective-permute-start(bf16[136,512]{1,0:T(8,128)(2,1)S(1)} %get-tuple-element.38), channel_id=1, source_target_pairs={{0,2},{1,3},{2,0},{3,1},{4,6},{5,7},{6,4},{7,5},{8,10},{9,11},{10,... | collective-permute-start | bytes 417800 | tf_op jit(solution)/shard_map/ppermute | solution.py:428
  17.5 0.0 collective-permute-done.2.refs_3_
  17.5 0.9 %short_part.1 = (bf16[96,512]{1,0:T(8,128)(2,1)S(1)}, bf16[96,512]{1,0:T(8,128)(2,1)S(1)}, bf16[96,512]{1,0:T(8,128)(2,1)S(1)}, bf16[96,512]{1,0:T(8,128)(2,1)S(1)}, f32[4,8,96]{2,1,0:T(8,128)S(1)}) custom-call(bf16[384,576]{1,0:T(8,128)(2,1)S(1)} %get-tuple-element.30.q.short_q_ref, f32[96,128]{1,0:T(8,128)S(1)} %get-tuple-element.31.m, ...), custom_call_target="tpu_custom_call" | custom-call | flops 427819008 | bytes 1179648 | tf_op jit(solution)/shard_map/short_part/pallas_call | solution.py:506
  18.4 2.7 %collective-permute-start.5 = (bf16[96,512]{1,0:T(8,128)(2,1)S(1)}, bf16[96,512]{1,0:T(8,128)(2,1)S(1)}, u32[]{:S(2)}, u32[]{:S(2)}) collective-permute-start(bf16[96,512]{1,0:T(8,128)(2,1)S(1)} %get-tuple-element.44), channel_id=1, source_target_pairs={{0,8},{1,9},{2,10},{3,11},{4,12},{5,13},{6,14},{7,15},{8,0},{9,1},... | collective-permute-start | bytes 294920 | tf_op jit(solution)/shard_map/ppermute | solution.py:428
  21.1 1.6 %collective-permute-start.4 = (bf16[96,512]{1,0:T(8,128)(2,1)S(1)}, bf16[96,512]{1,0:T(8,128)(2,1)S(1)}, u32[]{:S(2)}, u32[]{:S(2)}) collective-permute-start(bf16[96,512]{1,0:T(8,128)(2,1)S(1)} %get-tuple-element.43), channel_id=1, source_target_pairs={{0,4},{1,5},{2,6},{3,7},{4,0},{5,1},{6,2},{7,3},{8,12},{9,13},{10,... | collective-permute-start | bytes 294920 | tf_op jit(solution)/shard_map/ppermute | solution.py:428
  22.6 0.2 collective-permute-start.6
  22.9 0.0 collective-permute-done.3.refs_1_
  22.9 0.2 long_merge.1
  23.0 1.9 %collective-permute-start.8 = (bf16[40,512]{1,0:T(8,128)(2,1)S(1)}, bf16[40,512]{1,0:T(8,128)(2,1)S(1)}, u32[]{:S(2)}, u32[]{:S(2)}) collective-permute-start(bf16[40,512]{1,0:T(8,128)(2,1)S(1)} %get-tuple-element.49), channel_id=1, source_target_pairs={{0,8},{1,9},{2,10},{3,11},{4,12},{5,13},{6,14},{7,15},{8,0},{9,1},... | collective-permute-start | bytes 122888 | tf_op jit(solution)/shard_map/ppermute | solution.py:428
  24.9 1.9 %collective-permute-start.9 = (bf16[40,512]{1,0:T(8,128)(2,1)S(1)}, bf16[40,512]{1,0:T(8,128)(2,1)S(1)}, u32[]{:S(2)}, u32[]{:S(2)}) collective-permute-start(bf16[40,512]{1,0:T(8,128)(2,1)S(1)} %get-tuple-element.50), channel_id=1, source_target_pairs={{0,12},{1,13},{2,14},{3,15},{4,8},{5,9},{6,10},{7,11},{8,4},{9,5},... | collective-permute-start | bytes 122888 | tf_op jit(solution)/shard_map/ppermute | solution.py:428
  26.8 0.7 %collective-permute-done.5.refs_1_ = bf16[96,512]{1,0:T(8,128)(2,1)S(1)} collective-permute-done((bf16[96,512]{1,0:T(8,128)(2,1)S(1)}, bf16[96,512]{1,0:T(8,128)(2,1)S(1)}, u32[]{:S(2)}, u32[]{:S(2)}) %collective-permute-start.5) | collective-permute-done | bytes 98336 | tf_op jit(solution)/shard_map/ppermute | solution.py:428
  27.5 0.2 collective-permute-start.7
  27.6 0.0 copy-done
  27.6 1.1 %step_part.1 = (f32[128,512]{1,0:T(8,128)S(1)}, f32[8,128]{1,0:T(8,128)S(1)}) custom-call(s32[4]{0:T(128)S(1)} %copy-done.1, s32[4]{0:T(128)S(1)} %copy-done.2, bf16[256,576]{1,0:T(8,128)(2,1)S(1)} %get-tuple-element.29.q.long_q_ref, bf16[384,576]{1,0:T(8,128)(2,1)S(1)} %get-tuple-element.30.q.short_q_ref, bf16[4,4,576]{2,1,0:T(4,128)(2,1)S(1)} %copy-done, ...), custom_call_target="tpu_custom_call" | custom-call | bytes 262144 | tf_op jit(solution)/shard_map/step_part/pallas_call | solution.py:532
  28.8 4.9 %collective-permute-done.8.refs_4_ = bf16[40,512]{1,0:T(8,128)(2,1)S(1)} collective-permute-done((bf16[40,512]{1,0:T(8,128)(2,1)S(1)}, bf16[40,512]{1,0:T(8,128)(2,1)S(1)}, u32[]{:S(2)}, u32[]{:S(2)}) %collective-permute-start.8) | collective-permute-done | bytes 40992 | tf_op jit(solution)/shard_map/ppermute | solution.py:428
  33.7 0.0 collective-permute-done.9.refs_5_
  33.7 0.0 collective-permute-done.4.refs_0_
  33.7 0.0 collective-permute-done.6.refs_2_
  33.7 0.0 collective-permute-done.7.refs_3_
  33.7 0.9 %combine.1 = bf16[4,32,512]{2,1,0:T(8,128)(2,1)} custom-call(f32[8,128]{1,0:T(8,128)S(1)} %get-tuple-element.28.o, f32[128,512]{1,0:T(8,128)S(1)} %get-tuple-element.41.s, f32[8,128]{1,0:T(8,128)S(1)} %get-tuple-element.42.l, bf16[96,512]{1,0:T(8,128)(2,1)S(1)} %collective-permute-done.4.refs_0_, bf16[96,512]{1,0:T(8,128)(2,1)S(1)} %collective-permute-done.5.refs_1_, ...), custom_call_target="tpu_custom_call" | custom-call | bytes 524288 | tf_op jit(solution)/shard_map/combine/pallas_call | solution.py:550
Async XLA Ops:
  0.0 11.3 %copy-start.1 = (s32[4]{0:T(128)S(1)}, s32[4]{0:T(128)}, u32[]{:S(2)}) copy-start(s32[4]{0:T(128)} %lengths_ref.3) | copy-start | bytes 52
  0.0 11.3 %copy-start.2 = (s32[4]{0:T(128)S(1)}, s32[4]{0:T(128)}, u32[]{:S(2)}) copy-start(s32[4]{0:T(128)} %owners_ref.3) | copy-start | bytes 52
  0.0 27.6 %copy-start = (bf16[4,4,576]{2,1,0:T(4,128)(2,1)S(1)}, bf16[4,4,576]{2,1,0:T(4,128)(2,1)}, u32[]{:S(2)}) copy-start(bf16[4,4,576]{2,1,0:T(4,128)(2,1)} %step_ref.1) | copy-start | bytes 55300
  8.2 6.1 %collective-permute-start = (bf16[576,512]{1,0:T(8,128)(2,1)S(1)}, bf16[576,512]{1,0:T(8,128)(2,1)S(1)}, u32[]{:S(2)}, u32[]{:S(2)}) collective-permute-start(bf16[576,512]{1,0:T(8,128)(2,1)S(1)} %get-tuple-element.32.refs_0_), channel_id=1, source_target_pairs={{0,1},{1,0},{2,3},{3,2},{4,5},{5,4},{6,7},{7,6},{8,9},{9,8},{10,11... | collective-permute-start | bytes 1769480 | tf_op jit(solution)/shard_map/ppermute | solution.py:428
  8.7 7.0 %collective-permute-start.1 = (bf16[144,512]{1,0:T(8,128)(2,1)S(1)}, bf16[144,512]{1,0:T(8,128)(2,1)S(1)}, u32[]{:S(2)}, u32[]{:S(2)}) collective-permute-start(bf16[144,512]{1,0:T(8,128)(2,1)S(1)} %get-tuple-element.34), channel_id=1, source_target_pairs={{0,2},{1,3},{2,0},{3,1},{4,6},{5,7},{6,4},{7,5},{8,10},{9,11},{10,... | collective-permute-start | bytes 442376 | tf_op jit(solution)/shard_map/ppermute | solution.py:428
  15.7 1.8 %collective-permute-start.2 = (bf16[144,512]{1,0:T(8,128)(2,1)S(1)}, bf16[144,512]{1,0:T(8,128)(2,1)S(1)}, u32[]{:S(2)}, u32[]{:S(2)}) collective-permute-start(bf16[144,512]{1,0:T(8,128)(2,1)S(1)} %collective-permute-done.1.refs_2_), channel_id=1, source_target_pairs={{0,1},{1,0},{2,3},{3,2},{4,5},{5,4},{6,7},{7,6},{8,9},{9,8},{10,11... | collective-permute-start | bytes 442376 | tf_op jit(solution)/shard_map/ppermute | solution.py:428
  15.7 7.1 %collective-permute-start.3 = (bf16[136,512]{1,0:T(8,128)(2,1)S(1)}, bf16[136,512]{1,0:T(8,128)(2,1)S(1)}, u32[]{:S(2)}, u32[]{:S(2)}) collective-permute-start(bf16[136,512]{1,0:T(8,128)(2,1)S(1)} %get-tuple-element.38), channel_id=1, source_target_pairs={{0,2},{1,3},{2,0},{3,1},{4,6},{5,7},{6,4},{7,5},{8,10},{9,11},{10,... | collective-permute-start | bytes 417800 | tf_op jit(solution)/shard_map/ppermute | solution.py:428
  18.4 9.0 %collective-permute-start.5 = (bf16[96,512]{1,0:T(8,128)(2,1)S(1)}, bf16[96,512]{1,0:T(8,128)(2,1)S(1)}, u32[]{:S(2)}, u32[]{:S(2)}) collective-permute-start(bf16[96,512]{1,0:T(8,128)(2,1)S(1)} %get-tuple-element.44), channel_id=1, source_target_pairs={{0,8},{1,9},{2,10},{3,11},{4,12},{5,13},{6,14},{7,15},{8,0},{9,1},... | collective-permute-start | bytes 294920 | tf_op jit(solution)/shard_map/ppermute | solution.py:428
  21.1 12.6 %collective-permute-start.4 = (bf16[96,512]{1,0:T(8,128)(2,1)S(1)}, bf16[96,512]{1,0:T(8,128)(2,1)S(1)}, u32[]{:S(2)}, u32[]{:S(2)}) collective-permute-start(bf16[96,512]{1,0:T(8,128)(2,1)S(1)} %get-tuple-element.43), channel_id=1, source_target_pairs={{0,4},{1,5},{2,6},{3,7},{4,0},{5,1},{6,2},{7,3},{8,12},{9,13},{10,... | collective-permute-start | bytes 294920 | tf_op jit(solution)/shard_map/ppermute | solution.py:428
  22.6 11.1 %collective-permute-start.6 = (bf16[96,512]{1,0:T(8,128)(2,1)S(1)}, bf16[96,512]{1,0:T(8,128)(2,1)S(1)}, u32[]{:S(2)}, u32[]{:S(2)}) collective-permute-start(bf16[96,512]{1,0:T(8,128)(2,1)S(1)} %get-tuple-element.47), channel_id=1, source_target_pairs={{0,12},{1,13},{2,14},{3,15},{4,8},{5,9},{6,10},{7,11},{8,4},{9,5},... | collective-permute-start | bytes 294920 | tf_op jit(solution)/shard_map/ppermute | solution.py:428
  23.0 10.7 %collective-permute-start.8 = (bf16[40,512]{1,0:T(8,128)(2,1)S(1)}, bf16[40,512]{1,0:T(8,128)(2,1)S(1)}, u32[]{:S(2)}, u32[]{:S(2)}) collective-permute-start(bf16[40,512]{1,0:T(8,128)(2,1)S(1)} %get-tuple-element.49), channel_id=1, source_target_pairs={{0,8},{1,9},{2,10},{3,11},{4,12},{5,13},{6,14},{7,15},{8,0},{9,1},... | collective-permute-start | bytes 122888 | tf_op jit(solution)/shard_map/ppermute | solution.py:428
  24.9 8.8 %collective-permute-start.9 = (bf16[40,512]{1,0:T(8,128)(2,1)S(1)}, bf16[40,512]{1,0:T(8,128)(2,1)S(1)}, u32[]{:S(2)}, u32[]{:S(2)}) collective-permute-start(bf16[40,512]{1,0:T(8,128)(2,1)S(1)} %get-tuple-element.50), channel_id=1, source_target_pairs={{0,12},{1,13},{2,14},{3,15},{4,8},{5,9},{6,10},{7,11},{8,4},{9,5},... | collective-permute-start | bytes 122888 | tf_op jit(solution)/shard_map/ppermute | solution.py:428
  27.5 6.3 %collective-permute-start.7 = (bf16[40,512]{1,0:T(8,128)(2,1)S(1)}, bf16[40,512]{1,0:T(8,128)(2,1)S(1)}, u32[]{:S(2)}, u32[]{:S(2)}) collective-permute-start(bf16[40,512]{1,0:T(8,128)(2,1)S(1)} %get-tuple-element.48), channel_id=1, source_target_pairs={{0,4},{1,5},{2,6},{3,7},{4,0},{5,1},{6,2},{7,3},{8,12},{9,13},{10,... | collective-permute-start | bytes 122888 | tf_op jit(solution)/shard_map/ppermute | solution.py:428
